TPU v7x, 32 devices: a whole 2x2x4 slice. The times are simulated.
32 devices in a mesh: dp: 8 (over z, x), tensor: 4 (over y, core).
Axes of the slice: x: 2, y: 2, z: 4, core: 2. Of those that a mesh axis runs over, the one named last changes fastest.
Arguments:
- tokens: bfloat16 [2048, 4096], P('dp', 'tensor'), may hold values from -6 to 6
- out_grad: bfloat16 [2048, 4096], P('dp', 'tensor'), may hold values from -0.59765625 to 0.59765625
- w_in: bfloat16 [96, 128, 128], P('tensor'), may hold values from -0.25 to 0.25
- w_out: bfloat16 [96, 128, 128], P('tensor'), may hold values from -0.25 to 0.25
- block_rows: int32 [4, 24], P('tensor'), may hold values from -1 to 31, as said below
- block_cols: int32 [4, 24], P('tensor'), may hold values from -1 to 27, as said below
Outputs:
- in_grad: bfloat16 [2048, 4096], P('dp')
- win_grad: float32 [96, 16384], P('tensor', 'dp')
- wout_grad: float32 [96, 16384], P('tensor', 'dp')
Inputs may be any that keep to these rules, and one draw needn't show every extreme that they name: `block_rows`: -1 marks an empty slot; the live slots of one tensor index name distinct blocks; at least 12 slots of each tensor index are live, and all 24 slots of some tensor index are live. `block_cols`: -1 exactly where block_rows is -1.
All inputs are finite; a program needn't handle non-finite values.
Results may differ from a plain program's by a relative error of at most 0.02.
Values may be sent and summed in bfloat16 or wider, within the bound.
A program may use at most 64 MiB of HBM per device.

v0:
```python
import jax
import jax.numpy as jnp
from jax import lax
from jax.sharding import PartitionSpec as P

FF = 14336


highest = lax.Precision.HIGHEST
clip_limit = 4.0


def local(tokens, out_grad, w_in, w_out, block_rows, block_cols):
    bin_scale = 4194304.0 / lax.axis_size("dp")
    whole_tokens, whole_grad = (
        lax.all_gather(tokens, "tensor", axis=1, tiled=True),
        lax.all_gather(out_grad, "tensor", axis=1, tiled=True),
    )
    tok_count = whole_tokens.shape[0]
    width = whole_tokens.shape[1]
    side = w_in.shape[1]
    row_count = width // side
    col_count = FF // side // lax.axis_size("tensor")
    rows = block_rows[0]
    cols = block_cols[0]
    live = rows >= 0
    livef = live.astype(jnp.float32)
    safe_rows = jnp.where(live, rows, 0)
    safe_cols = jnp.where(live, cols, 0)
    col_hot = (safe_cols[:, None] == jnp.arange(col_count, dtype=jnp.int32)[None, :]).astype(
        jnp.float32
    ) * livef[:, None]
    row_hot = (safe_rows[:, None] == jnp.arange(row_count, dtype=jnp.int32)[None, :]).astype(
        jnp.float32
    ) * livef[:, None]
    in_blocks = whole_tokens.reshape(tok_count, row_count, side).transpose(1, 0, 2)
    grad_blocks = whole_grad.reshape(tok_count, row_count, side).transpose(1, 0, 2)
    picked = jnp.take(in_blocks, safe_rows, axis=0)
    picked_grad = jnp.take(grad_blocks, safe_rows, axis=0)
    slot_pre = jnp.einsum("stk,skh->sth", picked, w_in, preferred_element_type=jnp.float32)
    pre = jnp.einsum("sc,sth->cth", col_hot, slot_pre, precision=highest)
    hidden = jax.nn.silu(pre).astype(jnp.bfloat16)
    slot_back = jnp.einsum("std,shd->sth", picked_grad, w_out, preferred_element_type=jnp.float32)
    dhidden = jnp.einsum("sc,sth->cth", col_hot, slot_back, precision=highest)
    sigma = jax.nn.sigmoid(pre)
    dpre = (dhidden * sigma * (1.0 + pre * (1.0 - sigma))).astype(jnp.bfloat16)
    dpre_picked = jnp.take(dpre, safe_cols, axis=0)
    hidden_picked = jnp.take(hidden, safe_cols, axis=0)
    slot_terms = jnp.einsum("sth,sdh->std", dpre_picked, w_in, preferred_element_type=jnp.float32)
    partial_grad = jnp.einsum("sr,std->rtd", row_hot, slot_terms, precision=highest)
    summed = lax.psum(partial_grad.astype(jnp.bfloat16), "tensor")
    in_grad = summed.transpose(1, 0, 2).reshape(tok_count, width)
    grad_in = (
        jnp.einsum("stk,sth->skh", picked, dpre_picked, preferred_element_type=jnp.float32)
        * livef[:, None, None]
    )
    grad_out = (
        jnp.einsum("sth,std->shd", hidden_picked, picked_grad, preferred_element_type=jnp.float32)
        * livef[:, None, None]
    )
    slot_count = grad_in.shape[0]
    bins_in = jnp.floor(jnp.clip(grad_in, -clip_limit, clip_limit) * bin_scale).reshape(
        slot_count, side * side
    )
    bins_out = jnp.floor(jnp.clip(grad_out, -clip_limit, clip_limit) * bin_scale).reshape(
        slot_count, side * side
    )
    total_in, total_out = (
        lax.psum_scatter(
            bins_in.astype(jnp.bfloat16), "dp", scatter_dimension=1, tiled=True
        ).astype(jnp.float32),
        lax.psum_scatter(
            bins_out.astype(jnp.bfloat16), "dp", scatter_dimension=1, tiled=True
        ).astype(jnp.float32),
    )
    win_grad = total_in / bin_scale
    wout_grad = total_out / bin_scale
    return (in_grad, win_grad, wout_grad)


def solution(mesh):
    in_specs = (
        P("dp", "tensor"),
        P("dp", "tensor"),
        P("tensor", None, None),
        P("tensor", None, None),
        P("tensor", None),
        P("tensor", None),
    )
    out_specs = (P("dp", None), P("tensor", "dp"), P("tensor", "dp"))
    return jax.shard_map(local, mesh=mesh, in_specs=in_specs, out_specs=out_specs, check_vma=False)
```

profile of v0, /device:TPU:0, one launch (start us, length us, event | category | flops | bytes accessed | tf_op | source)
XLA Modules:
  0.0 286.4 jit_solution(4583814118207411598)
XLA Ops:
  7.3 2.1 copy.18
  9.4 0.0 all-gather.3.cloned.1.call-start
  9.5 1.0 copy.15
  10.5 0.0 reduce-scatter.3.cloned.1.call-start
  10.6 24.9 %all-gather.5.cloned.1.call-done = bf16[256,4096]{0,1:T(8,128)(2,1)} async-done(((bf16[256,1024]{0,1:T(8,128)(2,1)}), bf16[256,4096]{0,1:T(8,128)(2,1)}) %all-gather.5.cloned.1.call-update) | async-done | bytes 2097168 | tf_op jit(solution)/shard_map/all_gather | solution.py:16
  35.5 3.2 %copy.19 = bf16[256,32,128]{2,0,1:T(8,128)(2,1)S(1)} copy(bf16[256,32,128]{0,2,1:T(8,128)(2,1)} %bitcast.47) | data formatting | bytes 4194304 | tf_op jit(solution)/shard_map/reshape | solution.py:36
  38.7 21.0 %all-gather.3.cloned.1.call-done = bf16[256,4096]{0,1:T(8,128)(2,1)} async-done(((bf16[256,1024]{0,1:T(8,128)(2,1)}), bf16[256,4096]{0,1:T(8,128)(2,1)}) %all-gather.3.cloned.1.call-update) | async-done | bytes 2097168 | tf_op jit(solution)/shard_map/all_gather | solution.py:17
  59.7 4.1 %copy.16 = bf16[256,32,128]{2,0,1:T(8,128)(2,1)} copy(bf16[256,32,128]{0,2,1:T(8,128)(2,1)} %bitcast.48) | data formatting | bytes 4194304 | tf_op jit(solution)/shard_map/reshape | solution.py:37
  63.7 1.9 gather_fusion.1
  65.7 2.4 gather_fusion
  68.2 2.6 fusion.18
  70.8 7.9 %multiply_convert_fusion = (bf16[28,256,128]{2,0,1:T(8,128)(2,1)}, f32[28,256,128]{2,0,1:T(8,128)S(1)}) fusion(f32[24,256,128]{2,1,0:T(8,128)S(1)} %fusion.18, f32[24]{0:T(128)S(1)} %get-tuple-element.11, s32[24]{0:T(128)S(1)} %get-tuple-element.6), kind=kOutput, calls=%fused_computation.4 | convolution fusion | flops 268830016 | bytes 8650944 | tf_op jit(solution)/shard_map/sc,sth->cth/dot_general | solution.py:41
  78.7 0.6 fusion.17
  79.3 8.2 %multiply_convert_fusion.1 = bf16[28,256,128]{2,0,1:T(8,128)(2,1)S(1)} fusion(f32[28,256,128]{2,0,1:T(8,128)S(1)} %get-tuple-element.13, f32[24,256,128]{2,1,0:T(8,128)S(1)} %fusion.17, f32[24]{0:T(128)S(1)} %get-tuple-element.11, s32[24]{0:T(128)S(1)} %get-tuple-element.6), kind=kOutput, calls=%fused_computation.5 | convolution fusion | flops 272500032 | bytes 8650944 | tf_op jit(solution)/shard_map/sc,sth->cth/dot_general | solution.py:44
  87.5 0.7 copy.21
  88.2 2.0 gather_fusion.2
  90.1 2.8 floor_convert_fusion.1
  93.0 1.4 copy.48
  94.4 0.0 reduce-scatter.5.cloned.1.call-start
  94.4 2.3 copy.24
  96.8 1.9 gather_fusion.3
  98.7 2.8 floor_convert_fusion
  101.5 1.4 copy.47
  103.0 0.6 fusion.19
  103.7 6.9 %fusion.8 = bf16[32,256,128]{2,0,1:T(8,128)(2,1)S(1)} fusion(f32[24,256,128]{2,1,0:T(8,128)S(1)} %fusion.19, f32[24]{0:T(128)S(1)} %get-tuple-element.11, s32[24]{0:T(128)S(1)} %compare_select_fusion.3), kind=kOutput, calls=%fused_computation.14 | convolution fusion | flops 303040000 | bytes 5243072 | tf_op jit(solution)/shard_map/sr,std->rtd/dot_general | solution.py:50
  110.6 2.3 copy.46
  112.9 44.8 %reduce-scatter.3.cloned.1.call-done = bf16[24,2048]{1,0:T(8,128)(2,1)} async-done(((bf16[24,16384]{1,0:T(8,128)(2,1)}), bf16[24,2048]{1,0:T(8,128)(2,1)}) %reduce-scatter.3.cloned.1.call-update) | async-done | bytes 98320 | tf_op jit(solution)/shard_map/reduce_scatter | solution.py:69
  157.7 1.6 convert_multiply_fusion.1
  159.3 64.2 %reduce-scatter.5.cloned.1.call-done = bf16[24,2048]{1,0:T(8,128)(2,1)} async-done(((bf16[24,16384]{1,0:T(8,128)(2,1)}), bf16[24,2048]{1,0:T(8,128)(2,1)}) %reduce-scatter.5.cloned.1.call-update) | async-done | bytes 98320 | tf_op jit(solution)/shard_map/reduce_scatter | solution.py:72
  223.5 1.6 convert_multiply_fusion
  225.1 51.6 %all-reduce.2.cloned.1.call-done = bf16[256,4096]{1,0:T(8,128)(2,1)} async-done(((bf16[256,4096]{1,0:T(8,128)(2,1)}), bf16[256,4096]{1,0:T(8,128)(2,1)}) %all-reduce.2.cloned.1.call-update) | async-done | bytes 2097168 | tf_op jit(solution)/shard_map/psum | solution.py:51
  276.7 3.1 %copy.50 = bf16[256,4096]{1,0:T(8,128)(2,1)} copy(bf16[256,4096]{1,0:T(8,128)(2,1)} %all-reduce.2.cloned.1.call-done) | data formatting | bytes 4194304
  (26 shorter events, 0.2 us)
Async XLA Ops:
  7.2 61.0 %copy-start = (bf16[24,128,128]{2,1,0:T(8,128)(2,1)S(1)}, bf16[24,128,128]{2,1,0:T(8,128)(2,1)}, u32[]{:S(2)}) copy-start(bf16[24,128,128]{2,1,0:T(8,128)(2,1)} %param.12) | copy-start | bytes 2359300
  7.2 2.3 copy-start.4
  7.2 3.4 %copy-start.6 = (s32[1,24]{1,0:T(1,128)S(1)}, s32[1,24]{1,0:T(1,128)}, u32[]{:S(2)}) copy-start(s32[1,24]{1,0:T(1,128)} %param.14) | copy-start | bytes 292
  7.2 3.4 %copy-start.5 = (s32[1,24]{1,0:T(1,128)S(1)}, s32[1,24]{1,0:T(1,128)}, u32[]{:S(2)}) copy-start(s32[1,24]{1,0:T(1,128)} %param.15) | copy-start | bytes 292
  7.2 28.3 %all-gather.5.cloned.1.call-start = ((), (), s32[]{:S(2)}) async-start(), calls=%async_computation.3 | async-start | bytes 2621440 | tf_op jit(solution)/shard_map/all_gather | solution.py:16
  9.4 50.3 %all-gather.3.cloned.1.call-start = ((), (), s32[]{:S(2)}) async-start(), calls=%async_computation.2 | async-start | bytes 2621440 | tf_op jit(solution)/shard_map/all_gather | solution.py:17
  10.5 147.2 %reduce-scatter.3.cloned.1.call-start = ((), (), s32[]{:S(2)}) async-start(), calls=%async_computation.5 | async-start | bytes 884736 | tf_op jit(solution)/shard_map/reduce_scatter | solution.py:69
  68.1 10.5 %copy-start.2 = (bf16[24,256,128]{2,1,0:T(8,128)(2,1)}, bf16[24,256,128]{2,1,0:T(8,128)(2,1)S(1)}, u32[]{:S(2)}) copy-start(bf16[24,256,128]{2,1,0:T(8,128)(2,1)S(1)} %gather_fusion) | copy-start | bytes 4718596
  70.8 7.9 %copy-start.3 = (bf16[24,128,128]{2,1,0:T(8,128)(2,1)S(1)}, bf16[24,128,128]{2,1,0:T(8,128)(2,1)}, u32[]{:S(2)}) copy-start(bf16[24,128,128]{2,1,0:T(8,128)(2,1)} %param.13) | copy-start | bytes 2359300
  94.4 129.1 %reduce-scatter.5.cloned.1.call-start = ((), (), s32[]{:S(2)}) async-start(), calls=%async_computation.6 | async-start | bytes 884736 | tf_op jit(solution)/shard_map/reduce_scatter | solution.py:72
  101.5 1.5 copy-start.1
  103.0 173.8 %all-reduce.2.cloned.1.call-start = ((), (), s32[]{:S(2)}) async-start(), calls=%async_computation.4 | async-start | bytes 4194304 | tf_op jit(solution)/shard_map/psum | solution.py:51
Sparse Core Ops, SparseCore 0:
  10.2 25.2 all-gather.4
  37.1 22.5 all-gather.2
  94.5 63.1 reduce-scatter.2
  161.2 62.2 reduce-scatter.4
  226.3 50.3 all-reduce.1
where the time goes:
time: 287 us; the launch traced here: 286 us
  waiting for transfers between devices  207 us (72%)
  matrix products  32.4 us (11%)
  local copies, waits for them, and re-layouts  30 us (10%)
  between operations  14 us (5%)
  other arithmetic  3.2 us (1%)
    reduce_scatter x1, waiting for transfers between devices, local(): lax.psum_scatter(bins_out.astype(jnp.bfloat16), 'dp', scatter_dimension=1...  64.2 us
    psum x1, waiting for transfers between devices, local(): summed = lax.psum(partial_grad.astype(jnp.bfloat16), 'tensor')  51.6 us
    reduce_scatter x1, waiting for transfers between devices, local(): lax.psum_scatter(bins_in.astype(jnp.bfloat16), 'dp', scatter_dimension=1,...  44.8 us
    all_gather x1, waiting for transfers between devices, local(): lax.all_gather(tokens, 'tensor', axis=1, tiled=True)  24.9 us
    all_gather x1, waiting for transfers between devices, local(): lax.all_gather(out_grad, 'tensor', axis=1, tiled=True)  21 us
    unnamed x20, local copies, waits for them, and re-layouts  11.4 us
    dot_general x1, matrix products, local(): dhidden = jnp.einsum('sc,sth->cth', col_hot, slot_back, precision=highest)  8.16 us
    dot_general x1, matrix products, local(): pre = jnp.einsum('sc,sth->cth', col_hot, slot_pre, precision=highest)  7.89 us
  transfers between devices with their start and end apart: 5, of which 5 were waited for; matrix products, arithmetic and copies ran while one was open for 9% of the time, Pallas kernels for 0%

commit v1 on v0

v1 whole, which is shorter than its diff:
```python
import functools

import jax
import jax.numpy as jnp
from jax import lax
from jax.experimental import pallas as pl
from jax.experimental.pallas import tpu as pltpu
from jax.sharding import PartitionSpec as P

MESH = pl.DeviceIdType.MESH
BF, F32, I32 = jnp.bfloat16, jnp.float32, jnp.int32
CLIP = 4.0
UNROLL = 4


def dot(a, b, ca, cb):
    return lax.dot_general(a, b, (((ca,), (cb,)), ((), ())), preferred_element_type=F32)


def order_of(key, idx):
    equal = key[None, :] == key[:, None]
    earlier = idx[None, :] < idx[:, None]
    rank = jnp.sum(((key[None, :] < key[:, None]) | (equal & earlier)).astype(I32), 1)
    hot = rank[None, :] == idx[:, None]
    perm = jnp.sum(jnp.where(hot, idx[None, :], 0), 1)
    joins = jnp.any(equal & earlier, 1)
    same = jnp.sum(jnp.where(hot, joins[None, :].astype(I32), 0), 1)
    end = jnp.max(jnp.where(equal, rank[None, :], 0), 1)
    return rank, perm, same, end


def table(block_rows, block_cols, row_count):
    rows, cols = block_rows[0], block_cols[0]
    cap = rows.shape[0]
    idx = jnp.arange(cap, dtype=I32)
    live = rows >= 0
    _, perm_c, same_c, end_c = order_of(jnp.where(live, cols, (1 << 20) + idx), idx)
    rank_r, perm_r, same_r, _ = order_of(jnp.where(live, rows, (1 << 20) + idx), idx)
    safe = jnp.where(live, rows, 0)
    row_c = jnp.sum(jnp.where(perm_c[:, None] == idx[None, :], safe[None, :], 0), 1)
    hit = rows[None, :] == jnp.arange(row_count, dtype=I32)[:, None]
    last_r = jnp.max(jnp.where(hit, rank_r[None, :], 0), 1)
    has_r = jnp.any(hit, 1).astype(I32)
    lines = [
        perm_c,
        same_c,
        end_c,
        safe,
        row_c,
        live.astype(I32),
        perm_r,
        same_r,
        last_r,
        has_r,
    ]
    size = max(cap, row_count)
    return jnp.stack([jnp.pad(v, (0, size - v.shape[0])) for v in lines])


def kernel(
    n_dp, n_t,
    meta, tok_hbm, grad_hbm, win_hbm, wout_hbm,
    dx_out, gin_out, gout_out,
    tok0, tok1, grad0, grad1, tcut0, tcut1, gcut0, gcut1, win, wout, scan_p, scan_h, terms, rscan, hid, dpre,
    part, rsib, ysum, yrecv, res, stage_i, stage_o, xr_i, xr_o, zs_i, zs_o, zr_i, zr_o,
    ag_send, ag_recv, sib_send, sib_recv, loc, wloc, p_send, p_recv, r_send, r_recv,
    o_send, o_recv, o_loc, x_send, x_recv, z_send, z_recv,
):
    tok, grad = (tok0, tok1), (grad0, grad1)
    cap, side = win.shape[0], win.shape[1]
    half = tok0.shape[1]
    n_y, n_j = n_t // 2, n_dp // 2
    row_count = n_t * tok0.shape[2] // side
    span = side // n_dp
    wide = row_count * side // 2
    scale = 4194304.0 / n_dp
    d, t = lax.axis_index("dp"), lax.axis_index("tensor")
    c, y = lax.rem(t, 2), t // 2
    sib = y * 2 + (1 - c)
    b, j = lax.rem(d, 2), d // 2
    xpeer = j * 2 + (1 - b)

    def y_at(k):
        return lax.rem(y + k + n_y, n_y) * 2 + c

    def j_at(k):
        return lax.rem(j + k + n_j, n_j)

    barrier = pltpu.get_barrier_semaphore()
    peers = [{"tensor": sib}, {"dp": xpeer}]
    peers += [{"tensor": y_at(k)} for k in range(1, n_y)]
    peers += [{"dp": j_at(k) * 2 + b} for k in range(1, n_j)]
    for peer in peers:
        pl.semaphore_signal(barrier, inc=1, device_id=peer, device_id_type=MESH)

    def remote(src, dst, ss, rs, peer):
        return pltpu.make_async_remote_copy(
            src_ref=src, dst_ref=dst, send_sem=ss, recv_sem=rs, device_id=peer, device_id_type=MESH
        )

    hbm = (tok_hbm, grad_hbm)
    held = (tok, grad)
    cut = ((tcut0, tcut1), (gcut0, gcut1))

    def shard(a, h):
        return hbm[a].at[pl.ds(h * half, half), :]

    def ag_y(a, h, k):
        return remote(shard(a, h), held[a][h].at[t], ag_send.at[a, h, k - 1],
                      ag_recv.at[a, h, k - 1], {"tensor": y_at(k)})

    def ag_sib(a, h, k):
        src_t = y_at(-k)
        src = shard(a, h) if k == 0 else held[a][h].at[src_t]
        return remote(src, held[a][h].at[src_t], sib_send.at[a, h, k],
                      sib_recv.at[a, h, k], {"tensor": sib})

    def own(a, h):
        return pltpu.make_async_copy(shard(a, h), held[a][h].at[t], loc.at[a, h])

    weights = [pltpu.make_async_copy(win_hbm, win, wloc.at[0]),
               pltpu.make_async_copy(wout_hbm, wout, wloc.at[1])]

    def start_y(a, h):
        for k in range(1, n_y):
            ag_y(a, h, k).start()

    def pass_on(a, h):
        for k in range(1, n_y):
            ag_y(a, h, k).wait_recv()
            ag_sib(a, h, k).start()

    def settle(h):
        for a in range(2):
            own(a, h).wait()
            for k in range(n_y):
                ag_sib(a, h, k).wait_recv()

    for w in weights:
        w.start()
    for a in range(2):
        for h in range(2):
            own(a, h).start()
    pl.semaphore_wait(barrier, len(peers))
    start_y(0, 0)
    start_y(1, 0)
    for h in range(2):
        for a in range(2):
            ag_sib(a, h, 0).start()

    def split(h):
        per = tok0.shape[2] // side
        for a in range(2):
            def body(g, carry):
                for u in range(per):
                    cut[a][h][g * per + u] = held[a][h][g, :, u * side:(u + 1) * side]
                return carry
            lax.fori_loop(0, n_t, body, 0)

    def loop(count, body, carry):
        def outer(g, carry):
            for u in range(UNROLL):
                carry = body(g * UNROLL + u, carry)
            return carry
        return lax.fori_loop(0, count // UNROLL, outer, carry)

    def forward(h):
        def body(i, carry):
            acc_p, acc_h = carry
            s = meta[0, i]
            keep = meta[1, i].astype(F32)
            row = meta[4, i]
            acc_p = acc_p * keep + dot(cut[0][h][row], win[s], 1, 0)
            acc_h = acc_h * keep + dot(cut[1][h][row], wout[s], 1, 1)
            scan_p[i] = acc_p
            scan_h[i] = acc_h
            return acc_p, acc_h
        zero = jnp.zeros((half, side), F32)
        loop(cap, body, (zero, zero))

        def point(s, carry):
            e = meta[2, s]
            pre, dh = scan_p[e], scan_h[e]
            sigma = 1.0 / (1.0 + jnp.exp(-pre))
            hid[s, pl.ds(h * half, half), :] = (pre * sigma).astype(BF)
            dpre[s, pl.ds(h * half, half), :] = (
                dh * sigma * (1.0 + pre * (1.0 - sigma))
            ).astype(BF)
            return carry
        loop(cap, point, 0)

    def back(h):
        def term(s, carry):
            terms[s] = dot(dpre[s, pl.ds(h * half, half), :], win[s], 1, 1)
            return carry
        loop(cap, term, 0)

        def body(i, acc):
            acc = acc * meta[7, i].astype(F32) + terms[meta[6, i]]
            rscan[i] = acc
            return acc
        loop(cap, body, jnp.zeros((half, side), F32))
        for r in range(row_count):
            at, off = divmod(r * side, wide)
            part[h, at, :, pl.ds(off, side)] = (
                rscan[meta[8, r]] * meta[9, r].astype(F32)
            ).astype(BF)

    def exchange(h):
        return remote(part.at[h, 1 - c], rsib.at[h], p_send.at[h], p_recv.at[h], {"tensor": sib})

    def ring(h, k):
        return remote(ysum.at[h], yrecv.at[h, y], r_send.at[h, k - 1], r_recv.at[h, k - 1],
                      {"tensor": y_at(k)})

    def y_out(h):
        exchange(h).wait_recv()

        def rows(i, carry):
            at = pl.ds(pl.multiple_of(i * 16, 16), 16)
            ysum[h, at, :] = (
                part[h, c, at, :].astype(F32) + rsib[h, at, :].astype(F32)
            ).astype(BF)
            return carry
        lax.fori_loop(0, half // 16, rows, 0)
        for k in range(1, n_y):
            ring(h, k).start()

    def out_at(h):
        return dx_out.at[pl.ds(h * half, half), pl.ds(pl.multiple_of(c * wide, side), wide)]

    def out_sib(h):
        return remote(res.at[h], out_at(h), o_send.at[h], o_recv.at[h], {"tensor": sib})

    def out_own(h):
        return pltpu.make_async_copy(res.at[h], out_at(h), o_loc.at[h])

    def y_in(h):
        for k in range(1, n_y):
            ring(h, k).wait_recv()

        def rows(i, carry):
            at = pl.ds(pl.multiple_of(i * 16, 16), 16)
            mine = ysum[h, at, :].astype(F32)
            acc = jnp.zeros_like(mine)
            for g in range(n_y):
                acc = acc + jnp.where(y == g, mine, yrecv[h, g, at, :].astype(F32))
            res[h, at, :] = acc.astype(BF)
            return carry
        lax.fori_loop(0, half // 16, rows, 0)
        out_sib(h).start()
        out_own(h).start()

    stage, xr, zs, zr = (stage_i, stage_o), (xr_i, xr_o), (zs_i, zs_o), (zr_i, zr_o)
    g_out = (gin_out, gout_out)

    def wgrad(kind):
        def body(s, carry):
            row = meta[3, s]
            block = jnp.concatenate([cut[kind][0][row], cut[kind][1][row]], 0)
            g = dot(block, dpre[s], 0, 0) if kind == 0 else dot(hid[s], block, 0, 0)
            q = jnp.floor(jnp.clip(g, -CLIP, CLIP) * scale) * meta[5, s].astype(F32)
            q = q.astype(BF)
            for p in range(n_dp):
                stage[kind][p % 2, p // 2, s] = q[p * span:(p + 1) * span]
            return carry
        loop(cap, body, 0)

    def x_swap(kind):
        return remote(stage[kind].at[1 - b], xr[kind], x_send.at[kind], x_recv.at[kind],
                      {"dp": xpeer})

    def z_send_to(kind, k):
        return remote(zs[kind].at[j_at(k)], zr[kind].at[k - 1], z_send.at[kind, k - 1],
                      z_recv.at[kind, k - 1], {"dp": j_at(k) * 2 + b})

    def z_out(kind):
        x_swap(kind).wait_recv()
        for k in list(range(1, n_j)) + [0]:
            g = j_at(k)
            zs[kind][g] = (stage[kind][b, g].astype(F32) + xr[kind][g].astype(F32)).astype(BF)
            if k:
                z_send_to(kind, k).start()

    def z_in(kind):
        acc = zs[kind][j].astype(F32)
        for k in range(1, n_j):
            z_send_to(kind, k).wait_recv()
            acc = acc + zr[kind][k - 1].astype(F32)
        g_out[kind][...] = acc * (1.0 / scale)

    pass_on(0, 0)
    start_y(0, 1)
    pass_on(1, 0)
    start_y(1, 1)
    for w in weights:
        w.wait()
    settle(0)
    split(0)
    forward(0)
    back(0)
    exchange(0).start()
    y_out(0)
    pass_on(0, 1)
    pass_on(1, 1)
    settle(1)
    split(1)
    forward(1)
    wgrad(1)
    x_swap(1).start()
    wgrad(0)
    x_swap(0).start()
    back(1)
    exchange(1).start()
    y_out(1)
    z_out(1)
    z_out(0)
    y_in(0)
    z_in(1)
    y_in(1)
    z_in(0)
    for h in range(2):
        out_own(h).wait()
        out_sib(h).wait()
        exchange(h).wait_send()
        for a in range(2):
            for k in range(1, n_y):
                ag_y(a, h, k).wait_send()
            for k in range(n_y):
                ag_sib(a, h, k).wait_send()
        for k in range(1, n_y):
            ring(h, k).wait_send()
    for kind in range(2):
        x_swap(kind).wait_send()
        for k in range(1, n_j):
            z_send_to(kind, k).wait_send()


def local(n_dp, n_t, tokens, out_grad, w_in, w_out, block_rows, block_cols):
    tok_count, shard_width = tokens.shape
    cap, side = w_in.shape[0], w_in.shape[1]
    width = shard_width * n_t
    half, wide, span = tok_count // 2, width // 2, side // n_dp
    n_y, n_j = n_t // 2, n_dp // 2
    meta = table(block_rows, block_cols, width // side)
    vm = pltpu.VMEM
    dma = pltpu.SemaphoreType.DMA
    gathered = vm((n_t, half, shard_width), BF)
    cuts = vm((width // side, half, side), BF)
    blocks = vm((cap, side, side), BF)
    slots = vm((cap, half, side), F32)
    stage = vm((2, n_j, cap, span, side), BF)
    piece = vm((n_j, cap, span, side), BF)
    landing = vm((max(n_j - 1, 1), cap, span, side), BF)
    scratch = [
        gathered, gathered, gathered, gathered, cuts, cuts, cuts, cuts, blocks, blocks, slots, slots, slots, slots,
        vm((cap, tok_count, side), BF), vm((cap, tok_count, side), BF),
        vm((2, 2, half, wide), BF), vm((2, half, wide), BF), vm((2, half, wide), BF),
        vm((2, n_y, half, wide), BF), vm((2, half, wide), BF),
        stage, stage, piece, piece, piece, piece, landing, landing,
        dma((2, 2, n_y - 1)), dma((2, 2, n_y - 1)), dma((2, 2, n_y)), dma((2, 2, n_y)),
        dma((2, 2)), dma((2,)), dma((2,)), dma((2,)), dma((2, n_y - 1)), dma((2, n_y - 1)),
        dma((2,)), dma((2,)), dma((2,)), dma((2,)), dma((2,)),
        dma((2, n_j - 1)), dma((2, n_j - 1)),
    ]
    any_space = pl.BlockSpec(memory_space=pl.ANY)
    grads = jax.ShapeDtypeStruct((cap, span, side), F32)
    in_grad, win_grad, wout_grad = pl.pallas_call(
        functools.partial(kernel, n_dp, n_t),
        out_shape=(jax.ShapeDtypeStruct((tok_count, width), BF), grads, grads),
        in_specs=[pl.BlockSpec(memory_space=pltpu.SMEM)] + [any_space] * 4,
        out_specs=(any_space, pl.BlockSpec(memory_space=vm), pl.BlockSpec(memory_space=vm)),
        scratch_shapes=scratch,
        compiler_params=pltpu.CompilerParams(
            collective_id=0, has_side_effects=True, vmem_limit_bytes=56 * 1024 * 1024
        ),
        cost_estimate=pl.CostEstimate(
            flops=10 * cap * tok_count * side * side,
            bytes_accessed=8 * tok_count * width,
            transcendentals=cap * tok_count * side,
        ),
    )(meta, tokens, out_grad, w_in, w_out)
    return in_grad, win_grad.reshape(cap, span * side), wout_grad.reshape(cap, span * side)


def solution(mesh):
    in_specs = (
        P("dp", "tensor"),
        P("dp", "tensor"),
        P("tensor", None, None),
        P("tensor", None, None),
        P("tensor", None),
        P("tensor", None),
    )
    out_specs = (P("dp", None), P("tensor", "dp"), P("tensor", "dp"))
    body = functools.partial(local, mesh.shape["dp"], mesh.shape["tensor"])
    return jax.shard_map(body, mesh=mesh, in_specs=in_specs, out_specs=out_specs, check_vma=False)
```

time: 287 us -> 78.1 us (0.27)
  waiting for transfers between devices: 207 us -> 0 us
  Pallas kernels: 0 us -> 64.9 us
  matrix products: 32.4 us -> 0 us
  local copies, waits for them, and re-layouts: 30 us -> 7.71 us
  between operations: 14 us -> 0.69 us
    reduce_scatter x2 -> x0, waiting for transfers between devices: 109 us -> none  [the longest x1 64.2 us: local(): lax.psum_scatter(bins_out.astype(jnp.bfloat16), 'dp', scatter_dimension=1...]
    pallas_call x0 -> x1, Pallas kernels: none -> 64.9 us  [local(): pl.pallas_call(functools.partial(kernel, n_dp, n_t), out_shape=(jax.Shape...]
    psum x1 -> x0, waiting for transfers between devices: 51.6 us -> none  [local(): summed = lax.psum(partial_grad.astype(jnp.bfloat16), 'tensor')]
    all_gather x2 -> x0, waiting for transfers between devices: 45.8 us -> none  [the longest x1 24.9 us: local(): lax.all_gather(tokens, 'tensor', axis=1, tiled=True)]
    dot_general x8 -> x0, matrix products: 32.4 us -> none  [the longest x1 8.16 us: local(): dhidden = jnp.einsum('sc,sth->cth', col_hot, slot_back, precision=highest)]
    gather x4 -> x0, local copies, waits for them, and re-layouts: 8.29 us -> none  [the longest x1 2.44 us: local(): picked_grad = jnp.take(grad_blocks, safe_rows, axis=0)]
    reshape x2 -> x0, local copies, waits for them, and re-layouts: 7.28 us -> none  [the longest x1 4.06 us: local(): whole_grad.reshape(tok_count, row_count, side).transpose(1, 0, 2)]
    unnamed x20 -> x3, local copies, waits for them, and re-layouts: 11.4 us -> 6.46 us
  transfers between devices with their start and end apart: 5 -> 0, of which waited for: 5 -> 0; matrix products, arithmetic and copies ran while one was open for 9% -> 0% of each run, Pallas kernels for 0% -> 0%
where the time goes in v1:
time: 78.1 us; the launch traced here: 77.8 us
  Pallas kernels  64.9 us (83%)
  local copies, waits for them, and re-layouts  7.71 us (10%)
  other arithmetic  4.59 us (6%)
    pallas_call x1, Pallas kernels, local(): pl.pallas_call(functools.partial(kernel, n_dp, n_t), out_shape=(jax.Shape...  64.9 us
    unnamed x3, local copies, waits for them, and re-layouts  6.46 us

profile of v1, /device:TPU:0, one launch (start us, length us, event | category | flops | bytes accessed | tf_op | source)
XLA Modules:
  0.0 77.8 jit_solution(13794073467627106483)
XLA Ops:
  0.6 0.7 fusion.1
  1.4 0.7 broadcast_compare_fusion
  2.0 0.7 fusion.9
  2.7 0.7 fusion.8
  3.4 0.2 fusion.3
  3.6 0.2 fusion.4
  3.8 0.2 convert_reduce_fusion.1
  4.0 0.2 fusion
  4.2 0.2 select_reduce_fusion.3
  4.4 0.7 select_reduce_fusion
  5.2 0.1 select_reduce_fusion.1
  5.3 1.2 %stack.44.meta = s32[10,32]{1,0:T(8,128)} concatenate(s32[1,32]{1,0:T(1,128)S(1)} %pad_bitcast_fusion.6, s32[1,32]{1,0:T(1,128)S(1)} %pad_bitcast_fusion.5, s32[1,32]{1,0:T(1,128)S(1)} %pad_bitcast_fusion.4, s32[1,32]{1,0:T(1,128)S(1)} %pad_bitcast_fusion.3, s32[1,32]{1,0:T(1,128)S(1)} %pad_bitcast_fusion.2, s32[1,32]{1,0:T(1,128)S(1)} %get-tuple-element.21, ...), dimensions={0} | concatenate | bytes 2560 | tf_op jit(solution)/shard_map/stack | solution.py:57
  6.5 64.9 %shard_map.85 = (bf16[256,4096]{1,0:T(8,128)(2,1)}, f32[24,16,128]{2,1,0:T(8,128)}, f32[24,16,128]{2,1,0:T(8,128)}) custom-call(s32[10,32]{1,0:T(8,128)} %stack.44.meta, bf16[256,1024]{1,0:T(8,128)(2,1)} %tok_hbm.1, bf16[256,1024]{1,0:T(8,128)(2,1)} %grad_hbm.1, bf16[24,128,128]{2,1,0:T(8,128)(2,1)} %win_hbm.1, bf16[24,128,128]{2,1,0:T(8,128)(2,1)} %wout_hbm.1), custom_call_target="tpu_custom_call" | custom-call | flops 1006632960 | bytes 8388608 | tf_op jit(solution)/shard_map/pallas_call | solution.py:368
  71.4 1.7 %copy.14 = f32[3,8,16,128]{3,1,2,0:T(8,128)} copy(f32[3,8,16,128]{3,2,1,0:T(8,128)} %bitcast.48) | data formatting | bytes 393216
  73.1 1.7 %copy.13 = f32[3,8,16,128]{3,1,2,0:T(8,128)} copy(f32[3,8,16,128]{3,2,1,0:T(8,128)} %bitcast.47) | data formatting | bytes 393216
  74.7 3.1 %copy.16 = bf16[256,4096]{1,0:T(8,128)(2,1)} copy(bf16[256,4096]{1,0:T(8,128)(2,1)} %get-tuple-element.26) | data formatting | bytes 4194304
  (10 shorter events, 0.1 us)

commit v2 on v1

v2 whole, which is shorter than its diff:
```python
import functools

import jax
import jax.numpy as jnp
from jax import lax
from jax.experimental import pallas as pl
from jax.experimental.pallas import tpu as pltpu
from jax.sharding import PartitionSpec as P

MESH = pl.DeviceIdType.MESH
BF, F32, I32 = jnp.bfloat16, jnp.float32, jnp.int32
CLIP = 4.0
UNROLL = 4
PREV_COL, END_COL, ROW, LIVE, PREV_ROW, LAST = range(6)


def dot(a, b, ca, cb):
    return lax.dot_general(a, b, (((ca,), (cb,)), ((), ())), preferred_element_type=F32)


def loop(count, body):
    def outer(g, carry):
        for u in range(UNROLL):
            body(g * UNROLL + u)
        return carry

    lax.fori_loop(0, count // UNROLL, outer, 0)


def kernel(
    n_dp, n_t, chunk,
    rows, cols, tok_hbm, grad_hbm, win_hbm, wout_hbm,
    dx_out, gin_out, gout_out,
    table, tok0, tok1, grad0, grad1, tcut, gcut0, gcut1, win, wout, scan_p, scan_h, rscan,
    hid, gate, dpre, part, rsib, ysum, yrecv, res, stage, xr, zs, zr,
    ag_send, ag_recv, sib_send, sib_recv, loc, wloc, p_send, p_recv, r_send, r_recv,
    o_send, o_recv, o_loc, x_send, x_recv, z_send, z_recv,
):
    cap, side = win.shape[0], win.shape[1]
    half = tok0.shape[1]
    per = tok0.shape[2] // side
    n_y, n_j, n_c = n_t // 2, n_dp // 2, cap // chunk
    row_count = n_t * per
    span = side // n_dp
    wide = row_count * side // 2
    scale = 4194304.0 / n_dp
    d, t = lax.axis_index("dp"), lax.axis_index("tensor")
    c, y = lax.rem(t, 2), t // 2
    sib = y * 2 + (1 - c)
    b, j = lax.rem(d, 2), d // 2
    xpeer = j * 2 + (1 - b)

    def y_at(k):
        return lax.rem(y + k + n_y, n_y) * 2 + c

    def j_at(k):
        return lax.rem(j + k + n_j, n_j)

    barrier = pltpu.get_barrier_semaphore()
    peers = [{"tensor": sib}, {"dp": xpeer}]
    peers += [{"tensor": y_at(k)} for k in range(1, n_y)]
    peers += [{"dp": j_at(k) * 2 + b} for k in range(1, n_j)]
    for peer in peers:
        pl.semaphore_signal(barrier, inc=1, device_id=peer, device_id_type=MESH)

    def remote(src, dst, ss, rs, peer):
        return pltpu.make_async_remote_copy(
            src_ref=src, dst_ref=dst, send_sem=ss, recv_sem=rs, device_id=peer, device_id_type=MESH
        )

    hbm = (tok_hbm, grad_hbm)
    held = ((tok0, tok1), (grad0, grad1))

    def shard(a, h):
        return hbm[a].at[pl.ds(h * half, half), :]

    def ag_y(a, h, k):
        return remote(shard(a, h), held[a][h].at[t], ag_send.at[a, h, k - 1],
                      ag_recv.at[a, h, k - 1], {"tensor": y_at(k)})

    def ag_sib(a, h, k):
        src_t = y_at(-k)
        src = shard(a, h) if k == 0 else held[a][h].at[src_t]
        return remote(src, held[a][h].at[src_t], sib_send.at[a, h, k],
                      sib_recv.at[a, h, k], {"tensor": sib})

    def own(a, h):
        return pltpu.make_async_copy(shard(a, h), held[a][h].at[t], loc.at[a, h])

    weights = [pltpu.make_async_copy(win_hbm, win, wloc.at[0]),
               pltpu.make_async_copy(wout_hbm, wout, wloc.at[1])]

    def start_y(a, h):
        for k in range(1, n_y):
            ag_y(a, h, k).start()

    def pass_on(a, h):
        for k in range(1, n_y):
            ag_y(a, h, k).wait_recv()
            ag_sib(a, h, k).start()

    def settle(a, h):
        own(a, h).wait()
        for k in range(n_y):
            ag_sib(a, h, k).wait_recv()

        def split(g, carry):
            for u in range(per):
                block = held[a][h][g, :, u * side:(u + 1) * side]
                if a == 0:
                    tcut[g * per + u, h * half:(h + 1) * half, :] = block
                else:
                    (gcut0, gcut1)[h][g * per + u] = block
            return carry

        lax.fori_loop(0, n_t, split, 0)

    def tables():
        def of_slot(s, carry):
            col, row = cols[0, s], rows[0, s]
            prev_col, prev_row, end_col = I32(cap), I32(cap), I32(0)
            for q in range(cap):
                same_col, same_row = cols[0, q] == col, rows[0, q] == row
                prev_col = jnp.where(same_col & (q < s), q, prev_col)
                prev_row = jnp.where(same_row & (q < s), q, prev_row)
                end_col = jnp.where(same_col, q, end_col)
            table[PREV_COL, s] = prev_col
            table[PREV_ROW, s] = prev_row
            table[END_COL, s] = end_col
            table[ROW, s] = jnp.maximum(row, 0)
            table[LIVE, s] = jnp.where(row >= 0, 1, 0)
            return carry

        def of_row(r, carry):
            last = I32(cap)
            for q in range(cap):
                last = jnp.where(rows[0, q] == r, q, last)
            table[LAST, r] = last
            return carry

        lax.fori_loop(0, cap, of_slot, 0)
        lax.fori_loop(0, row_count, of_row, 0)

    def forward():
        def body(s):
            term = dot(tcut[table[ROW, s]], win[s], 1, 0)
            scan_p[s] = term + scan_p[table[PREV_COL, s]]

        loop(cap, body)

        def point(s):
            pre = scan_p[table[END_COL, s]]
            sigma = 1.0 / (1.0 + jnp.exp(-pre))
            hid[s] = (pre * sigma).astype(BF)
            gate[s] = sigma * (1.0 + pre * (1.0 - sigma))

        loop(cap, point)

    def backward(h):
        at = pl.ds(h * half, half)

        def body(s):
            term = dot((gcut0, gcut1)[h][table[ROW, s]], wout[s], 1, 1)
            scan_h[s] = term + scan_h[table[PREV_COL, s]]

        loop(cap, body)

        def point(s):
            dpre[s, at, :] = (scan_h[table[END_COL, s]] * gate[s, at, :]).astype(BF)

        loop(cap, point)

        def term(s):
            rscan[s] = dot(dpre[s, at, :], win[s], 1, 1) + rscan[table[PREV_ROW, s]]

        loop(cap, term)
        for r in range(row_count):
            at_half, off = divmod(r * side, wide)
            part[h, at_half, :, pl.ds(off, side)] = rscan[table[LAST, r]].astype(BF)

    def exchange(h):
        return remote(part.at[h, 1 - c], rsib.at[h], p_send.at[h], p_recv.at[h], {"tensor": sib})

    def ring(h, k):
        return remote(ysum.at[h], yrecv.at[h, y], r_send.at[h, k - 1], r_recv.at[h, k - 1],
                      {"tensor": y_at(k)})

    def y_out(h):
        exchange(h).wait_recv()

        def band(i, carry):
            at = pl.ds(pl.multiple_of(i * 16, 16), 16)
            ysum[h, at, :] = (
                part[h, c, at, :].astype(F32) + rsib[h, at, :].astype(F32)
            ).astype(BF)
            return carry

        lax.fori_loop(0, half // 16, band, 0)
        for k in range(1, n_y):
            ring(h, k).start()

    def out_at(h):
        return dx_out.at[pl.ds(h * half, half), pl.ds(pl.multiple_of(c * wide, side), wide)]

    def out_sib(h):
        return remote(res.at[h], out_at(h), o_send.at[h], o_recv.at[h], {"tensor": sib})

    def out_own(h):
        return pltpu.make_async_copy(res.at[h], out_at(h), o_loc.at[h])

    def y_in(h):
        for k in range(1, n_y):
            ring(h, k).wait_recv()

        def band(i, carry):
            at = pl.ds(pl.multiple_of(i * 16, 16), 16)
            mine = ysum[h, at, :].astype(F32)
            acc = jnp.zeros_like(mine)
            for g in range(n_y):
                acc = acc + jnp.where(y == g, mine, yrecv[h, g, at, :].astype(F32))
            res[h, at, :] = acc.astype(BF)
            return carry

        lax.fori_loop(0, half // 16, band, 0)
        out_sib(h).start()
        out_own(h).start()

    g_out = (gin_out, gout_out)

    def x_swap(kind, n):
        q = kind * n_c + n
        return remote(stage.at[q, 1 - b], xr.at[q], x_send.at[q], x_recv.at[q], {"dp": xpeer})

    def wgrad(kind, n):
        def body(i):
            s = n * chunk + i
            row = table[ROW, s]
            if kind == 0:
                g = dot(tcut[row], dpre[s], 0, 0)
            else:
                g = dot(hid[s], jnp.concatenate([gcut0[row], gcut1[row]], 0), 0, 0)
            bins = jnp.floor(jnp.clip(g, -CLIP, CLIP) * scale) * table[LIVE, s].astype(F32)
            bins = bins.astype(BF)
            for p in range(n_dp):
                stage[kind * n_c + n, p % 2, p // 2, i] = bins[p * span:(p + 1) * span]

        loop(chunk, body)
        x_swap(kind, n).start()

    def z_copy(kind, n, k):
        q = kind * n_c + n
        return remote(zs.at[q, j_at(k)], zr.at[q, k - 1], z_send.at[q, k - 1],
                      z_recv.at[q, k - 1], {"dp": j_at(k) * 2 + b})

    def z_out(kind, n):
        q = kind * n_c + n
        x_swap(kind, n).wait_recv()
        for k in list(range(1, n_j)) + [0]:
            g = j_at(k)
            zs[q, g] = (stage[q, b, g].astype(F32) + xr[q, g].astype(F32)).astype(BF)
            if k:
                z_copy(kind, n, k).start()

    def z_in(kind, n):
        q = kind * n_c + n
        acc = zs[q, j].astype(F32)
        for k in range(1, n_j):
            z_copy(kind, n, k).wait_recv()
            acc = acc + zr[q, k - 1].astype(F32)
        acc = acc * (1.0 / scale)
        for r in range(span):
            g_out[kind][n * chunk:(n + 1) * chunk, r * side:(r + 1) * side] = acc[:, r, :]

    for w in weights:
        w.start()
    for a in range(2):
        for h in range(2):
            own(a, h).start()
    pl.semaphore_wait(barrier, len(peers))
    start_y(0, 0)
    start_y(0, 1)
    for a in range(2):
        for h in range(2):
            ag_sib(a, h, 0).start()
    tables()
    scan_p[cap] = jnp.zeros(scan_p.shape[1:], F32)
    scan_h[cap] = jnp.zeros(scan_h.shape[1:], F32)
    rscan[cap] = jnp.zeros(rscan.shape[1:], F32)
    pass_on(0, 0)
    start_y(1, 0)
    pass_on(0, 1)
    start_y(1, 1)
    for w in weights:
        w.wait()
    settle(0, 0)
    settle(0, 1)
    forward()
    pass_on(1, 0)
    settle(1, 0)
    backward(0)
    exchange(0).start()
    pass_on(1, 1)
    y_out(0)
    settle(1, 1)
    for n in range(n_c):
        wgrad(1, n)
    backward(1)
    exchange(1).start()
    z_out(1, 0)
    for n in range(n_c):
        wgrad(0, n)
        if n == 0:
            y_out(1)
        if n + 1 < n_c:
            z_out(1, n + 1)
    z_out(0, 0)
    y_in(0)
    for n in range(1, n_c):
        z_out(0, n)
    for n in range(n_c):
        z_in(1, n)
    y_in(1)
    for n in range(n_c):
        z_in(0, n)
    for h in range(2):
        out_own(h).wait()
        out_sib(h).wait()
        exchange(h).wait_send()
        for a in range(2):
            for k in range(1, n_y):
                ag_y(a, h, k).wait_send()
            for k in range(n_y):
                ag_sib(a, h, k).wait_send()
        for k in range(1, n_y):
            ring(h, k).wait_send()
    for kind in range(2):
        for n in range(n_c):
            x_swap(kind, n).wait_send()
            for k in range(1, n_j):
                z_copy(kind, n, k).wait_send()


def hand_over(dx, gin, gout, dx_out, gin_out, gout_out, sem):
    pieces = sem.shape[0] - 2
    band = dx.shape[0] // pieces
    copies = [
        pltpu.make_async_copy(dx.at[pl.ds(i * band, band)], dx_out.at[pl.ds(i * band, band)],
                              sem.at[i])
        for i in range(pieces)
    ]
    copies.append(pltpu.make_async_copy(gin, gin_out, sem.at[pieces]))
    copies.append(pltpu.make_async_copy(gout, gout_out, sem.at[pieces + 1]))
    for copy in copies:
        copy.start()
    for copy in copies:
        copy.wait()


def local(n_dp, n_t, tokens, out_grad, w_in, w_out, block_rows, block_cols):
    tok_count, shard_width = tokens.shape
    cap, side = w_in.shape[0], w_in.shape[1]
    width = shard_width * n_t
    row_count = width // side
    half, wide, span = tok_count // 2, width // 2, side // n_dp
    n_y, n_j = n_t // 2, n_dp // 2
    chunk = 8 if cap % 8 == 0 else cap
    n_q = 2 * (cap // chunk)
    vm, dma = pltpu.VMEM, pltpu.SemaphoreType.DMA
    gathered = vm((n_t, half, shard_width), BF)
    blocks = vm((cap, side, side), BF)
    sums = vm((cap + 1, half, side), F32)
    piece = vm((n_q, n_j, chunk, span, side), BF)
    scratch = [
        pltpu.SMEM((6, max(cap, row_count)), I32),
        gathered, gathered, gathered, gathered,
        vm((row_count, tok_count, side), BF),
        vm((row_count, half, side), BF), vm((row_count, half, side), BF),
        blocks, blocks, vm((cap + 1, tok_count, side), F32), sums, sums,
        vm((cap, tok_count, side), BF), vm((cap, tok_count, side), F32),
        vm((cap, tok_count, side), BF),
        vm((2, 2, half, wide), BF), vm((2, half, wide), BF), vm((2, half, wide), BF),
        vm((2, n_y, half, wide), BF), vm((2, half, wide), BF),
        vm((n_q, 2, n_j, chunk, span, side), BF), piece, piece,
        vm((n_q, max(n_j - 1, 1), chunk, span, side), BF),
        dma((2, 2, n_y - 1)), dma((2, 2, n_y - 1)), dma((2, 2, n_y)), dma((2, 2, n_y)),
        dma((2, 2)), dma((2,)), dma((2,)), dma((2,)), dma((2, n_y - 1)), dma((2, n_y - 1)),
        dma((2,)), dma((2,)), dma((2,)), dma((n_q,)), dma((n_q,)),
        dma((n_q, n_j - 1)), dma((n_q, n_j - 1)),
    ]
    any_space = pl.BlockSpec(memory_space=pl.ANY)
    smem, vmem = pl.BlockSpec(memory_space=pltpu.SMEM), pl.BlockSpec(memory_space=vm)
    shapes = (
        jax.ShapeDtypeStruct((tok_count, width), BF),
        jax.ShapeDtypeStruct((cap, span * side), F32),
        jax.ShapeDtypeStruct((cap, span * side), F32),
    )
    results = pl.pallas_call(
        functools.partial(kernel, n_dp, n_t, chunk),
        out_shape=shapes,
        in_specs=[smem] * 2 + [any_space] * 4,
        out_specs=(any_space, vmem, vmem),
        scratch_shapes=scratch,
        compiler_params=pltpu.CompilerParams(
            collective_id=0, has_side_effects=True, vmem_limit_bytes=56 * 1024 * 1024
        ),
        cost_estimate=pl.CostEstimate(
            flops=10 * cap * tok_count * side * side,
            bytes_accessed=8 * tok_count * width,
            transcendentals=cap * tok_count * side,
        ),
    )(block_rows, block_cols, tokens, out_grad, w_in, w_out)
    return pl.pallas_call(
        hand_over,
        out_shape=shapes,
        in_specs=[any_space] * 3,
        out_specs=(any_space,) * 3,
        scratch_shapes=[dma((10,))],
    )(*results)


def solution(mesh):
    in_specs = (
        P("dp", "tensor"),
        P("dp", "tensor"),
        P("tensor", None, None),
        P("tensor", None, None),
        P("tensor", None),
        P("tensor", None),
    )
    out_specs = (P("dp", None), P("tensor", "dp"), P("tensor", "dp"))
    body = functools.partial(local, mesh.shape["dp"], mesh.shape["tensor"])
    return jax.shard_map(body, mesh=mesh, in_specs=in_specs, out_specs=out_specs, check_vma=False)
```

time: 78.1 us -> 136 us (1.74)
  Pallas kernels: 64.9 us -> 135 us
  local copies, waits for them, and re-layouts: 7.71 us -> 0 us
  other arithmetic: 4.59 us -> 0 us
    pallas_call x1 -> x2, Pallas kernels: 64.9 us -> 135 us  [the longest x1 76.6 us: local(): pl.pallas_call(hand_over, out_shape=shapes, in_specs=[any_space] * 3, out...]
    unnamed x3 -> x0, local copies, waits for them, and re-layouts: 6.46 us -> none
where the time goes in v2:
time: 136 us
  Pallas kernels  135 us (99%)
    pallas_call x1, Pallas kernels, local(): pl.pallas_call(hand_over, out_shape=shapes, in_specs=[any_space] * 3, out...  76.6 us
    pallas_call x1, Pallas kernels, local(): pl.pallas_call(functools.partial(kernel, n_dp, n_t, chunk), out_shape=sha...  58.6 us

profile of v2, /device:TPU:0, one launch (start us, length us, event | category | flops | bytes accessed | tf_op | source)
XLA Modules:
  0.0 135.9 jit_solution(16304912815058845143)
XLA Ops:
  0.6 58.6 %shard_map.85 = (bf16[256,4096]{1,0:T(8,128)(2,1)}, f32[24,2048]{1,0:T(8,128)}, f32[24,2048]{1,0:T(8,128)}) custom-call(s32[1,24]{1,0:T(1,128)} %rows.1, s32[1,24]{1,0:T(1,128)} %cols.1, bf16[256,1024]{1,0:T(8,128)(2,1)} %tok_hbm.1, bf16[256,1024]{1,0:T(8,128)(2,1)} %grad_hbm.1, bf16[24,128,128]{2,1,0:T(8,128)(2,1)} %win_hbm.1, bf16[24,128,128]{2,1,0:T(8,128)(2,1)} %wout_hbm.1), custom_call_target="tpu_custom_call" | custom-call | flops 1006632960 | bytes 8388608 | tf_op jit(solution)/shard_map/pallas_call | solution.py:397
  59.2 76.6 %shard_map.86 = (bf16[256,4096]{1,0:T(8,128)(2,1)}, f32[24,2048]{1,0:T(8,128)}, f32[24,2048]{1,0:T(8,128)}) custom-call(bf16[256,4096]{1,0:T(8,128)(2,1)} %get-tuple-element.6.dx, f32[24,2048]{1,0:T(8,128)} %get-tuple-element.7.gin, f32[24,2048]{1,0:T(8,128)} %get-tuple-element.8.gout), custom_call_target="tpu_custom_call" | custom-call | tf_op jit(solution)/shard_map/pallas_call | solution.py:412

commit v3 on v2

--- a/solution.py
+++ b/solution.py
@@ -32,7 +32,7 @@
     rows, cols, tok_hbm, grad_hbm, win_hbm, wout_hbm,
     dx_out, gin_out, gout_out,
     table, tok0, tok1, grad0, grad1, tcut, gcut0, gcut1, win, wout, scan_p, scan_h, rscan,
-    hid, gate, dpre, part, rsib, ysum, yrecv, res, stage, xr, zs, zr,
+    tok_t, hid_t, gate, dpre, part, rsib, ysum, yrecv, res, stage, xr, zs, zr,
     ag_send, ag_recv, sib_send, sib_recv, loc, wloc, p_send, p_recv, r_send, r_recv,
     o_send, o_recv, o_loc, x_send, x_recv, z_send, z_recv,
 ):
@@ -143,7 +143,9 @@
 
     def forward():
         def body(s):
-            term = dot(tcut[table[ROW, s]], win[s], 1, 0)
+            block = tcut[table[ROW, s]]
+            tok_t[s] = block.T
+            term = dot(block, win[s], 1, 0)
             scan_p[s] = term + scan_p[table[PREV_COL, s]]
 
         loop(cap, body)
@@ -151,12 +153,12 @@
         def point(s):
             pre = scan_p[table[END_COL, s]]
             sigma = 1.0 / (1.0 + jnp.exp(-pre))
-            hid[s] = (pre * sigma).astype(BF)
+            hid_t[s] = (pre * sigma).astype(BF).T
             gate[s] = sigma * (1.0 + pre * (1.0 - sigma))
 
         loop(cap, point)
 
-    def backward(h):
+    def backward(h, between=None):
         at = pl.ds(h * half, half)
 
         def body(s):
@@ -169,6 +171,9 @@
             dpre[s, at, :] = (scan_h[table[END_COL, s]] * gate[s, at, :]).astype(BF)
 
         loop(cap, point)
+
+        if between is not None:
+            between()
 
         def term(s):
             rscan[s] = dot(dpre[s, at, :], win[s], 1, 1) + rscan[table[PREV_ROW, s]]
@@ -234,11 +239,11 @@
     def wgrad(kind, n):
         def body(i):
             s = n * chunk + i
-            row = table[ROW, s]
             if kind == 0:
-                g = dot(tcut[row], dpre[s], 0, 0)
+                g = dot(tok_t[s], dpre[s], 1, 0)
             else:
-                g = dot(hid[s], jnp.concatenate([gcut0[row], gcut1[row]], 0), 0, 0)
+                row = table[ROW, s]
+                g = dot(hid_t[s], jnp.concatenate([gcut0[row], gcut1[row]], 0), 1, 0)
             bins = jnp.floor(jnp.clip(g, -CLIP, CLIP) * scale) * table[LIVE, s].astype(F32)
             bins = bins.astype(BF)
             for p in range(n_dp):
@@ -304,9 +309,8 @@
     settle(1, 1)
     for n in range(n_c):
         wgrad(1, n)
-    backward(1)
+    backward(1, lambda: z_out(1, 0))
     exchange(1).start()
-    z_out(1, 0)
     for n in range(n_c):
         wgrad(0, n)
         if n == 0:
@@ -340,19 +344,20 @@
                 z_copy(kind, n, k).wait_send()
 
 
-def hand_over(dx, gin, gout, dx_out, gin_out, gout_out, sem):
-    pieces = sem.shape[0] - 2
+def hand_over(dx, gin, gout, dx_out, gin_out, gout_out, dx_held, gin_held, gout_held, sem_in, sem_out):
+    pieces = sem_in.shape[0] - 2
     band = dx.shape[0] // pieces
-    copies = [
-        pltpu.make_async_copy(dx.at[pl.ds(i * band, band)], dx_out.at[pl.ds(i * band, band)],
-                              sem.at[i])
-        for i in range(pieces)
-    ]
-    copies.append(pltpu.make_async_copy(gin, gin_out, sem.at[pieces]))
-    copies.append(pltpu.make_async_copy(gout, gout_out, sem.at[pieces + 1]))
-    for copy in copies:
+    at = [pl.ds(i * band, band) for i in range(pieces)]
+    legs = [(dx.at[w], dx_held.at[w], dx_out.at[w]) for w in at]
+    legs += [(gin, gin_held, gin_out), (gout, gout_held, gout_out)]
+    arrive = [pltpu.make_async_copy(a, h, sem_in.at[i]) for i, (a, h, _) in enumerate(legs)]
+    leave = [pltpu.make_async_copy(h, o, sem_out.at[i]) for i, (_, h, o) in enumerate(legs)]
+    for copy in arrive:
         copy.start()
-    for copy in copies:
+    for first, second in zip(arrive, leave):
+        first.wait()
+        second.start()
+    for copy in leave:
         copy.wait()
 
 
@@ -376,7 +381,8 @@
         vm((row_count, tok_count, side), BF),
         vm((row_count, half, side), BF), vm((row_count, half, side), BF),
         blocks, blocks, vm((cap + 1, tok_count, side), F32), sums, sums,
-        vm((cap, tok_count, side), BF), vm((cap, tok_count, side), F32),
+        vm((cap, side, tok_count), BF), vm((cap, side, tok_count), BF),
+        vm((cap, tok_count, side), F32),
         vm((cap, tok_count, side), BF),
         vm((2, 2, half, wide), BF), vm((2, half, wide), BF), vm((2, half, wide), BF),
         vm((2, n_y, half, wide), BF), vm((2, half, wide), BF),
@@ -414,7 +420,8 @@
         out_shape=shapes,
         in_specs=[any_space] * 3,
         out_specs=(any_space,) * 3,
-        scratch_shapes=[dma((10,))],
+        scratch_shapes=[vm(v.shape, v.dtype) for v in shapes] + [dma((10,)), dma((10,))],
+        compiler_params=pltpu.CompilerParams(vmem_limit_bytes=56 * 1024 * 1024),
     )(*results)
 
 

time: 136 us -> 62.1 us (0.46)
  Pallas kernels: 135 us -> 61.3 us
    pallas_call x1, Pallas kernels: 76.6 us -> 2.56 us  [local(): pl.pallas_call(hand_over, out_shape=shapes, in_specs=[any_space] * 3, out...]
where the time goes in v3:
time: 62.1 us; the launch traced here: 61.9 us
  Pallas kernels  61.3 us (99%)
  between operations  0.64 us (1%)
    pallas_call x1, Pallas kernels, local(): pl.pallas_call(functools.partial(kernel, n_dp, n_t, chunk), out_shape=sha...  58.7 us
    pallas_call x1, Pallas kernels, local(): pl.pallas_call(hand_over, out_shape=shapes, in_specs=[any_space] * 3, out...  2.56 us

profile of v3, /device:TPU:0, one launch (start us, length us, event | category | flops | bytes accessed | tf_op | source)
XLA Modules:
  0.0 61.9 jit_solution(12575420838841354945)
XLA Ops:
  0.6 58.7 %shard_map.85 = (bf16[256,4096]{1,0:T(8,128)(2,1)}, f32[24,2048]{1,0:T(8,128)}, f32[24,2048]{1,0:T(8,128)}) custom-call(s32[1,24]{1,0:T(1,128)} %rows.1, s32[1,24]{1,0:T(1,128)} %cols.1, bf16[256,1024]{1,0:T(8,128)(2,1)} %tok_hbm.1, bf16[256,1024]{1,0:T(8,128)(2,1)} %grad_hbm.1, bf16[24,128,128]{2,1,0:T(8,128)(2,1)} %win_hbm.1, bf16[24,128,128]{2,1,0:T(8,128)(2,1)} %wout_hbm.1), custom_call_target="tpu_custom_call" | custom-call | flops 1006632960 | bytes 8388608 | tf_op jit(solution)/shard_map/pallas_call | solution.py:403
  59.4 2.6 %shard_map.86 = (bf16[256,4096]{1,0:T(8,128)(2,1)}, f32[24,2048]{1,0:T(8,128)}, f32[24,2048]{1,0:T(8,128)}) custom-call(bf16[256,4096]{1,0:T(8,128)(2,1)} %get-tuple-element.6.dx, f32[24,2048]{1,0:T(8,128)} %get-tuple-element.7.gin, f32[24,2048]{1,0:T(8,128)} %get-tuple-element.8.gout), custom_call_target="tpu_custom_call" | custom-call | tf_op jit(solution)/shard_map/pallas_call | solution.py:418

commit v4 on v3

--- a/solution.py
+++ b/solution.py
@@ -27,11 +27,22 @@
     lax.fori_loop(0, count // UNROLL, outer, 0)
 
 
+def loop_pairs(count, make, use):
+    def outer(g, carry):
+        at = [g * UNROLL + u for u in range(UNROLL)]
+        made = [make(i) for i in at]
+        for i, value in zip(at, made):
+            use(i, value)
+        return carry
+
+    lax.fori_loop(0, count // UNROLL, outer, 0)
+
+
 def kernel(
     n_dp, n_t, chunk,
     rows, cols, tok_hbm, grad_hbm, win_hbm, wout_hbm,
     dx_out, gin_out, gout_out,
-    table, tok0, tok1, grad0, grad1, tcut, gcut0, gcut1, win, wout, scan_p, scan_h, rscan,
+    table, tok0, tok1, grad0, grad1, tcut0, tcut1, gcut0, gcut1, win, wout, scan, rscan,
     tok_t, hid_t, gate, dpre, part, rsib, ysum, yrecv, res, stage, xr, zs, zr,
     ag_send, ag_recv, sib_send, sib_recv, loc, wloc, p_send, p_recv, r_send, r_recv,
     o_send, o_recv, o_loc, x_send, x_recv, z_send, z_recv,
@@ -70,6 +81,7 @@
 
     hbm = (tok_hbm, grad_hbm)
     held = ((tok0, tok1), (grad0, grad1))
+    cut = ((tcut0, tcut1), (gcut0, gcut1))
 
     def shard(a, h):
         return hbm[a].at[pl.ds(h * half, half), :]
@@ -106,30 +118,25 @@
 
         def split(g, carry):
             for u in range(per):
-                block = held[a][h][g, :, u * side:(u + 1) * side]
-                if a == 0:
-                    tcut[g * per + u, h * half:(h + 1) * half, :] = block
-                else:
-                    (gcut0, gcut1)[h][g * per + u] = block
+                cut[a][h][g * per + u] = held[a][h][g, :, u * side:(u + 1) * side]
             return carry
 
         lax.fori_loop(0, n_t, split, 0)
 
     def tables():
-        def of_slot(s, carry):
+        for s in range(cap):
             col, row = cols[0, s], rows[0, s]
-            prev_col, prev_row, end_col = I32(cap), I32(cap), I32(0)
-            for q in range(cap):
-                same_col, same_row = cols[0, q] == col, rows[0, q] == row
-                prev_col = jnp.where(same_col & (q < s), q, prev_col)
-                prev_row = jnp.where(same_row & (q < s), q, prev_row)
-                end_col = jnp.where(same_col, q, end_col)
+            prev_col, prev_row, end_col = I32(cap), I32(cap), I32(s)
+            for q in range(s):
+                prev_col = jnp.where(cols[0, q] == col, q, prev_col)
+                prev_row = jnp.where(rows[0, q] == row, q, prev_row)
+            for q in range(s + 1, cap):
+                end_col = jnp.where(cols[0, q] == col, q, end_col)
             table[PREV_COL, s] = prev_col
             table[PREV_ROW, s] = prev_row
             table[END_COL, s] = end_col
             table[ROW, s] = jnp.maximum(row, 0)
             table[LIVE, s] = jnp.where(row >= 0, 1, 0)
-            return carry
 
         def of_row(r, carry):
             last = I32(cap)
@@ -138,47 +145,54 @@
             table[LAST, r] = last
             return carry
 
-        lax.fori_loop(0, cap, of_slot, 0)
         lax.fori_loop(0, row_count, of_row, 0)
 
-    def forward():
-        def body(s):
-            block = tcut[table[ROW, s]]
-            tok_t[s] = block.T
-            term = dot(block, win[s], 1, 0)
-            scan_p[s] = term + scan_p[table[PREV_COL, s]]
-
-        loop(cap, body)
+    def forward(h):
+        at = slice(h * half, (h + 1) * half)
+
+        def make(s):
+            block = cut[0][h][table[ROW, s]]
+            return block.T, dot(block, win[s], 1, 0)
+
+        def use(s, made):
+            tok_t[s, :, at] = made[0]
+            scan[s] = made[1] + scan[table[PREV_COL, s]]
+
+        loop_pairs(cap, make, use)
 
         def point(s):
-            pre = scan_p[table[END_COL, s]]
+            pre = scan[table[END_COL, s]]
             sigma = 1.0 / (1.0 + jnp.exp(-pre))
-            hid_t[s] = (pre * sigma).astype(BF).T
-            gate[s] = sigma * (1.0 + pre * (1.0 - sigma))
+            hid_t[s, :, at] = (pre * sigma).astype(BF).T
+            gate[s, at, :] = sigma * (1.0 + pre * (1.0 - sigma))
 
         loop(cap, point)
 
     def backward(h, between=None):
         at = pl.ds(h * half, half)
 
-        def body(s):
-            term = dot((gcut0, gcut1)[h][table[ROW, s]], wout[s], 1, 1)
-            scan_h[s] = term + scan_h[table[PREV_COL, s]]
-
-        loop(cap, body)
+        def make(s):
+            return dot(cut[1][h][table[ROW, s]], wout[s], 1, 1)
+
+        def use(s, made):
+            scan[s] = made + scan[table[PREV_COL, s]]
+
+        loop_pairs(cap, make, use)
 
         def point(s):
-            dpre[s, at, :] = (scan_h[table[END_COL, s]] * gate[s, at, :]).astype(BF)
+            dpre[s, at, :] = (scan[table[END_COL, s]] * gate[s, at, :]).astype(BF)
 
         loop(cap, point)
-
         if between is not None:
             between()
 
-        def term(s):
-            rscan[s] = dot(dpre[s, at, :], win[s], 1, 1) + rscan[table[PREV_ROW, s]]
-
-        loop(cap, term)
+        def make_term(s):
+            return dot(dpre[s, at, :], win[s], 1, 1)
+
+        def use_term(s, made):
+            rscan[s] = made + rscan[table[PREV_ROW, s]]
+
+        loop_pairs(cap, make_term, use_term)
         for r in range(row_count):
             at_half, off = divmod(r * side, wide)
             part[h, at_half, :, pl.ds(off, side)] = rscan[table[LAST, r]].astype(BF)
@@ -237,19 +251,20 @@
         return remote(stage.at[q, 1 - b], xr.at[q], x_send.at[q], x_recv.at[q], {"dp": xpeer})
 
     def wgrad(kind, n):
-        def body(i):
+        def make(i):
             s = n * chunk + i
             if kind == 0:
-                g = dot(tok_t[s], dpre[s], 1, 0)
-            else:
-                row = table[ROW, s]
-                g = dot(hid_t[s], jnp.concatenate([gcut0[row], gcut1[row]], 0), 1, 0)
-            bins = jnp.floor(jnp.clip(g, -CLIP, CLIP) * scale) * table[LIVE, s].astype(F32)
-            bins = bins.astype(BF)
+                return dot(tok_t[s], dpre[s], 1, 0)
+            row = table[ROW, s]
+            return dot(hid_t[s], jnp.concatenate([gcut0[row], gcut1[row]], 0), 1, 0)
+
+        def use(i, g):
+            live = table[LIVE, n * chunk + i].astype(F32)
+            bins = (jnp.floor(jnp.clip(g, -CLIP, CLIP) * scale) * live).astype(BF)
             for p in range(n_dp):
                 stage[kind * n_c + n, p % 2, p // 2, i] = bins[p * span:(p + 1) * span]
 
-        loop(chunk, body)
+        loop_pairs(chunk, make, use)
         x_swap(kind, n).start()
 
     def z_copy(kind, n, k):
@@ -283,29 +298,29 @@
             own(a, h).start()
     pl.semaphore_wait(barrier, len(peers))
     start_y(0, 0)
-    start_y(0, 1)
     for a in range(2):
         for h in range(2):
             ag_sib(a, h, 0).start()
     tables()
-    scan_p[cap] = jnp.zeros(scan_p.shape[1:], F32)
-    scan_h[cap] = jnp.zeros(scan_h.shape[1:], F32)
+    start_y(0, 1)
+    scan[cap] = jnp.zeros(scan.shape[1:], F32)
     rscan[cap] = jnp.zeros(rscan.shape[1:], F32)
     pass_on(0, 0)
     start_y(1, 0)
-    pass_on(0, 1)
-    start_y(1, 1)
     for w in weights:
         w.wait()
     settle(0, 0)
+    forward(0)
+    pass_on(0, 1)
+    start_y(1, 1)
     settle(0, 1)
-    forward()
+    forward(1)
     pass_on(1, 0)
     settle(1, 0)
     backward(0)
     exchange(0).start()
+    y_out(0)
     pass_on(1, 1)
-    y_out(0)
     settle(1, 1)
     for n in range(n_c):
         wgrad(1, n)
@@ -372,15 +387,14 @@
     n_q = 2 * (cap // chunk)
     vm, dma = pltpu.VMEM, pltpu.SemaphoreType.DMA
     gathered = vm((n_t, half, shard_width), BF)
+    cuts = vm((row_count, half, side), BF)
     blocks = vm((cap, side, side), BF)
     sums = vm((cap + 1, half, side), F32)
     piece = vm((n_q, n_j, chunk, span, side), BF)
     scratch = [
         pltpu.SMEM((6, max(cap, row_count)), I32),
         gathered, gathered, gathered, gathered,
-        vm((row_count, tok_count, side), BF),
-        vm((row_count, half, side), BF), vm((row_count, half, side), BF),
-        blocks, blocks, vm((cap + 1, tok_count, side), F32), sums, sums,
+        cuts, cuts, cuts, cuts, blocks, blocks, sums, sums,
         vm((cap, side, tok_count), BF), vm((cap, side, tok_count), BF),
         vm((cap, tok_count, side), F32),
         vm((cap, tok_count, side), BF),

time: 62.1 us -> 62.5 us (level)
  no operation moved by 1% of the time
where the time goes in v4:
time: 62.5 us; the launch traced here: 62.3 us
  Pallas kernels  61.7 us (99%)
  between operations  0.64 us (1%)
    pallas_call x1, Pallas kernels, local(): pl.pallas_call(functools.partial(kernel, n_dp, n_t, chunk), out_shape=sha...  59.1 us
    pallas_call x1, Pallas kernels, local(): pl.pallas_call(hand_over, out_shape=shapes, in_specs=[any_space] * 3, out...  2.56 us

profile of v4, /device:TPU:0, one launch (start us, length us, event | category | flops | bytes accessed | tf_op | source)
XLA Modules:
  0.0 62.3 jit_solution(17725337491822683869)
XLA Ops:
  0.6 59.1 %shard_map.85 = (bf16[256,4096]{1,0:T(8,128)(2,1)}, f32[24,2048]{1,0:T(8,128)}, f32[24,2048]{1,0:T(8,128)}) custom-call(s32[1,24]{1,0:T(1,128)} %rows.1, s32[1,24]{1,0:T(1,128)} %cols.1, bf16[256,1024]{1,0:T(8,128)(2,1)} %tok_hbm.1, bf16[256,1024]{1,0:T(8,128)(2,1)} %grad_hbm.1, bf16[24,128,128]{2,1,0:T(8,128)(2,1)} %win_hbm.1, bf16[24,128,128]{2,1,0:T(8,128)(2,1)} %wout_hbm.1), custom_call_target="tpu_custom_call" | custom-call | flops 1006632960 | bytes 8388608 | tf_op jit(solution)/shard_map/pallas_call | solution.py:417
  59.8 2.6 %shard_map.86 = (bf16[256,4096]{1,0:T(8,128)(2,1)}, f32[24,2048]{1,0:T(8,128)}, f32[24,2048]{1,0:T(8,128)}) custom-call(bf16[256,4096]{1,0:T(8,128)(2,1)} %get-tuple-element.6.dx, f32[24,2048]{1,0:T(8,128)} %get-tuple-element.7.gin, f32[24,2048]{1,0:T(8,128)} %get-tuple-element.8.gout), custom_call_target="tpu_custom_call" | custom-call | tf_op jit(solution)/shard_map/pallas_call | solution.py:432

commit v5 on v4

--- a/solution.py
+++ b/solution.py
@@ -200,49 +200,61 @@
     def exchange(h):
         return remote(part.at[h, 1 - c], rsib.at[h], p_send.at[h], p_recv.at[h], {"tensor": sib})
 
-    def ring(h, k):
-        return remote(ysum.at[h], yrecv.at[h, y], r_send.at[h, k - 1], r_recv.at[h, k - 1],
-                      {"tensor": y_at(k)})
+    parts = 2
+    piece = half // parts
+
+    def ring(h, p, k):
+        at = pl.ds(p * piece, piece)
+        return remote(ysum.at[h, at, :], yrecv.at[h, y, at, :], r_send.at[h, p, k - 1],
+                      r_recv.at[h, p, k - 1], {"tensor": y_at(k)})
+
+    def bands(p, body):
+        def band(i, carry):
+            body(pl.ds(pl.multiple_of(p * piece + i * 16, 16), 16))
+            return carry
+
+        lax.fori_loop(0, piece // 16, band, 0)
 
     def y_out(h):
         exchange(h).wait_recv()
 
-        def band(i, carry):
-            at = pl.ds(pl.multiple_of(i * 16, 16), 16)
+        def add(at):
             ysum[h, at, :] = (
                 part[h, c, at, :].astype(F32) + rsib[h, at, :].astype(F32)
             ).astype(BF)
-            return carry
-
-        lax.fori_loop(0, half // 16, band, 0)
-        for k in range(1, n_y):
-            ring(h, k).start()
-
-    def out_at(h):
-        return dx_out.at[pl.ds(h * half, half), pl.ds(pl.multiple_of(c * wide, side), wide)]
-
-    def out_sib(h):
-        return remote(res.at[h], out_at(h), o_send.at[h], o_recv.at[h], {"tensor": sib})
-
-    def out_own(h):
-        return pltpu.make_async_copy(res.at[h], out_at(h), o_loc.at[h])
+
+        for p in range(parts):
+            bands(p, add)
+            for k in range(1, n_y):
+                ring(h, p, k).start()
+
+    def out_at(h, p):
+        at = pl.ds(h * half + p * piece, piece)
+        return dx_out.at[at, pl.ds(pl.multiple_of(c * wide, side), wide)]
+
+    def done(h, p):
+        return res.at[h, pl.ds(p * piece, piece), :]
+
+    def out_sib(h, p):
+        return remote(done(h, p), out_at(h, p), o_send.at[h, p], o_recv.at[h, p], {"tensor": sib})
+
+    def out_own(h, p):
+        return pltpu.make_async_copy(done(h, p), out_at(h, p), o_loc.at[h, p])
 
     def y_in(h):
-        for k in range(1, n_y):
-            ring(h, k).wait_recv()
-
-        def band(i, carry):
-            at = pl.ds(pl.multiple_of(i * 16, 16), 16)
+        def add(at):
             mine = ysum[h, at, :].astype(F32)
             acc = jnp.zeros_like(mine)
             for g in range(n_y):
                 acc = acc + jnp.where(y == g, mine, yrecv[h, g, at, :].astype(F32))
             res[h, at, :] = acc.astype(BF)
-            return carry
-
-        lax.fori_loop(0, half // 16, band, 0)
-        out_sib(h).start()
-        out_own(h).start()
+
+        for p in range(parts):
+            for k in range(1, n_y):
+                ring(h, p, k).wait_recv()
+            bands(p, add)
+            out_sib(h, p).start()
+            out_own(h, p).start()
 
     g_out = (gin_out, gout_out)
 
@@ -342,38 +354,23 @@
     for n in range(n_c):
         z_in(0, n)
     for h in range(2):
-        out_own(h).wait()
-        out_sib(h).wait()
+        for p in range(parts):
+            out_own(h, p).wait()
+            out_sib(h, p).wait()
         exchange(h).wait_send()
         for a in range(2):
             for k in range(1, n_y):
                 ag_y(a, h, k).wait_send()
             for k in range(n_y):
                 ag_sib(a, h, k).wait_send()
-        for k in range(1, n_y):
-            ring(h, k).wait_send()
+        for p in range(parts):
+            for k in range(1, n_y):
+                ring(h, p, k).wait_send()
     for kind in range(2):
         for n in range(n_c):
             x_swap(kind, n).wait_send()
             for k in range(1, n_j):
                 z_copy(kind, n, k).wait_send()
-
-
-def hand_over(dx, gin, gout, dx_out, gin_out, gout_out, dx_held, gin_held, gout_held, sem_in, sem_out):
-    pieces = sem_in.shape[0] - 2
-    band = dx.shape[0] // pieces
-    at = [pl.ds(i * band, band) for i in range(pieces)]
-    legs = [(dx.at[w], dx_held.at[w], dx_out.at[w]) for w in at]
-    legs += [(gin, gin_held, gin_out), (gout, gout_held, gout_out)]
-    arrive = [pltpu.make_async_copy(a, h, sem_in.at[i]) for i, (a, h, _) in enumerate(legs)]
-    leave = [pltpu.make_async_copy(h, o, sem_out.at[i]) for i, (_, h, o) in enumerate(legs)]
-    for copy in arrive:
-        copy.start()
-    for first, second in zip(arrive, leave):
-        first.wait()
-        second.start()
-    for copy in leave:
-        copy.wait()
 
 
 def local(n_dp, n_t, tokens, out_grad, w_in, w_out, block_rows, block_cols):
@@ -403,18 +400,14 @@
         vm((n_q, 2, n_j, chunk, span, side), BF), piece, piece,
         vm((n_q, max(n_j - 1, 1), chunk, span, side), BF),
         dma((2, 2, n_y - 1)), dma((2, 2, n_y - 1)), dma((2, 2, n_y)), dma((2, 2, n_y)),
-        dma((2, 2)), dma((2,)), dma((2,)), dma((2,)), dma((2, n_y - 1)), dma((2, n_y - 1)),
-        dma((2,)), dma((2,)), dma((2,)), dma((n_q,)), dma((n_q,)),
+        dma((2, 2)), dma((2,)), dma((2,)), dma((2,)), dma((2, 2, n_y - 1)),
+        dma((2, 2, n_y - 1)), dma((2, 2)), dma((2, 2)), dma((2, 2)), dma((n_q,)), dma((n_q,)),
         dma((n_q, n_j - 1)), dma((n_q, n_j - 1)),
     ]
     any_space = pl.BlockSpec(memory_space=pl.ANY)
     smem, vmem = pl.BlockSpec(memory_space=pltpu.SMEM), pl.BlockSpec(memory_space=vm)
-    shapes = (
-        jax.ShapeDtypeStruct((tok_count, width), BF),
-        jax.ShapeDtypeStruct((cap, span * side), F32),
-        jax.ShapeDtypeStruct((cap, span * side), F32),
-    )
-    results = pl.pallas_call(
+    shapes = (vm((tok_count, width), BF),) + (vm((cap, span * side), F32),) * 2
+    return pl.pallas_call(
         functools.partial(kernel, n_dp, n_t, chunk),
         out_shape=shapes,
         in_specs=[smem] * 2 + [any_space] * 4,
@@ -429,14 +422,6 @@
             transcendentals=cap * tok_count * side,
         ),
     )(block_rows, block_cols, tokens, out_grad, w_in, w_out)
-    return pl.pallas_call(
-        hand_over,
-        out_shape=shapes,
-        in_specs=[any_space] * 3,
-        out_specs=(any_space,) * 3,
-        scratch_shapes=[vm(v.shape, v.dtype) for v in shapes] + [dma((10,)), dma((10,))],
-        compiler_params=pltpu.CompilerParams(vmem_limit_bytes=56 * 1024 * 1024),
-    )(*results)
 
 
 def solution(mesh):

time: 62.5 us -> 62 us (level)
  Pallas kernels: 61.7 us -> 58.5 us
  local copies, waits for them, and re-layouts: 0 us -> 2.67 us
    unnamed x0 -> x3, local copies, waits for them, and re-layouts: none -> 2.67 us
    pallas_call x1 -> x0, Pallas kernels: 2.56 us -> none  [local(): pl.pallas_call(hand_over, out_shape=shapes, in_specs=[any_space] * 3, out...]
    pallas_call x1, Pallas kernels: 59.1 us -> 58.5 us  [local(): pl.pallas_call(functools.partial(kernel, n_dp, n_t, chunk), out_shape=sha...]
where the time goes in v5:
time: 62 us; the launch traced here: 61.8 us
  Pallas kernels  58.5 us (94%)
  local copies, waits for them, and re-layouts  2.67 us (4%)
  between operations  0.64 us (1%)
    pallas_call x1, Pallas kernels, local(): pl.pallas_call(functools.partial(kernel, n_dp, n_t, chunk), out_shape=sha...  58.5 us
    unnamed x3, local copies, waits for them, and re-layouts  2.67 us

profile of v5, /device:TPU:0, one launch (start us, length us, event | category | flops | bytes accessed | tf_op | source)
XLA Modules:
  0.0 61.8 jit_solution(17887397837934124034)
XLA Ops:
  0.6 58.5 %shard_map.85 = (bf16[256,4096]{1,0:T(8,128)(2,1)S(1)}, f32[24,2048]{1,0:T(8,128)S(1)}, f32[24,2048]{1,0:T(8,128)S(1)}) custom-call(s32[1,24]{1,0:T(1,128)} %rows.1, s32[1,24]{1,0:T(1,128)} %cols.1, bf16[256,1024]{1,0:T(8,128)(2,1)} %tok_hbm.1, bf16[256,1024]{1,0:T(8,128)(2,1)} %grad_hbm.1, bf16[24,128,128]{2,1,0:T(8,128)(2,1)} %win_hbm.1, ...), custom_call_target="tpu_custom_call" | custom-call | flops 1006632960 | bytes 8388608 | tf_op jit(solution)/shard_map/pallas_call | solution.py:410
  59.1 1.3 %copy.12 = bf16[256,4096]{1,0:T(8,128)(2,1)} copy(bf16[256,4096]{1,0:T(8,128)(2,1)S(1)} %get-tuple-element.3) | data formatting | bytes 4194304
  60.4 0.7 %copy.13 = f32[24,2048]{1,0:T(8,128)} copy(f32[24,2048]{1,0:T(8,128)S(1)} %get-tuple-element.4) | data formatting | bytes 393216
  61.1 0.7 %copy.14 = f32[24,2048]{1,0:T(8,128)} copy(f32[24,2048]{1,0:T(8,128)S(1)} %get-tuple-element.5) | data formatting | bytes 393216

commit v6 on v5

--- a/solution.py
+++ b/solution.py
@@ -336,18 +336,19 @@
     settle(1, 1)
     for n in range(n_c):
         wgrad(1, n)
-    backward(1, lambda: z_out(1, 0))
+
+    def between():
+        for n in range(n_c):
+            z_out(1, n)
+            wgrad(0, n)
+
+    backward(1, between)
     exchange(1).start()
-    for n in range(n_c):
-        wgrad(0, n)
-        if n == 0:
-            y_out(1)
-        if n + 1 < n_c:
-            z_out(1, n + 1)
     z_out(0, 0)
-    y_in(0)
+    y_out(1)
     for n in range(1, n_c):
         z_out(0, n)
+    y_in(0)
     for n in range(n_c):
         z_in(1, n)
     y_in(1)
@@ -371,6 +372,18 @@
             x_swap(kind, n).wait_send()
             for k in range(1, n_j):
                 z_copy(kind, n, k).wait_send()
+
+
+def hand_over(dx, gin, gout, dx_out, gin_out, gout_out, sem):
+    pieces = sem.shape[0] - 2
+    band = dx.shape[0] // pieces
+    at = [pl.ds(i * band, band) for i in range(pieces)]
+    legs = [(dx.at[w], dx_out.at[w]) for w in at] + [(gin, gin_out), (gout, gout_out)]
+    copies = [pltpu.make_async_copy(a, b, sem.at[i]) for i, (a, b) in enumerate(legs)]
+    for copy in copies:
+        copy.start()
+    for copy in copies:
+        copy.wait()
 
 
 def local(n_dp, n_t, tokens, out_grad, w_in, w_out, block_rows, block_cols):
@@ -407,7 +420,7 @@
     any_space = pl.BlockSpec(memory_space=pl.ANY)
     smem, vmem = pl.BlockSpec(memory_space=pltpu.SMEM), pl.BlockSpec(memory_space=vm)
     shapes = (vm((tok_count, width), BF),) + (vm((cap, span * side), F32),) * 2
-    return pl.pallas_call(
+    results = pl.pallas_call(
         functools.partial(kernel, n_dp, n_t, chunk),
         out_shape=shapes,
         in_specs=[smem] * 2 + [any_space] * 4,
@@ -422,6 +435,13 @@
             transcendentals=cap * tok_count * side,
         ),
     )(block_rows, block_cols, tokens, out_grad, w_in, w_out)
+    return pl.pallas_call(
+        hand_over,
+        out_shape=tuple(jax.ShapeDtypeStruct(v.shape, v.dtype) for v in results),
+        in_specs=[any_space] * 3,
+        out_specs=(any_space,) * 3,
+        scratch_shapes=[dma((6,))],
+    )(*results)
 
 
 def solution(mesh):

time: 62 us -> 143 us (2.31)
  Pallas kernels: 58.5 us -> 140 us
    pallas_call x0 -> x1, Pallas kernels: none -> 76.6 us  [local(): pl.pallas_call(hand_over, out_shape=tuple((jax.ShapeDtypeStruct(v.shape,...]
    pallas_call x1, Pallas kernels: 58.5 us -> 63 us  [local(): pl.pallas_call(functools.partial(kernel, n_dp, n_t, chunk), out_shape=sha...]
where the time goes in v6:
time: 143 us
  Pallas kernels  140 us (98%)
  local copies, waits for them, and re-layouts  2.67 us (2%)
    pallas_call x1, Pallas kernels, local(): pl.pallas_call(hand_over, out_shape=tuple((jax.ShapeDtypeStruct(v.shape,...  76.6 us
    pallas_call x1, Pallas kernels, local(): pl.pallas_call(functools.partial(kernel, n_dp, n_t, chunk), out_shape=sha...  63 us

profile of v6, /device:TPU:0, one launch (start us, length us, event | category | flops | bytes accessed | tf_op | source)
XLA Modules:
  0.0 142.9 jit_solution(16113627671742174131)
XLA Ops:
  0.6 63.0 %shard_map.85 = (bf16[256,4096]{1,0:T(8,128)(2,1)S(1)}, f32[24,2048]{1,0:T(8,128)S(1)}, f32[24,2048]{1,0:T(8,128)S(1)}) custom-call(s32[1,24]{1,0:T(1,128)} %rows.1, s32[1,24]{1,0:T(1,128)} %cols.1, bf16[256,1024]{1,0:T(8,128)(2,1)} %tok_hbm.1, bf16[256,1024]{1,0:T(8,128)(2,1)} %grad_hbm.1, bf16[24,128,128]{2,1,0:T(8,128)(2,1)} %win_hbm.1, ...), custom_call_target="tpu_custom_call" | custom-call | flops 1006632960 | bytes 8388608 | tf_op jit(solution)/shard_map/pallas_call | solution.py:423
  63.7 0.0 copy-start
  63.7 1.3 copy-done
  65.0 0.0 copy-start.1
  65.0 0.7 copy-done.1
  65.7 0.0 copy-start.2
  65.7 0.7 copy-done.2
  66.3 76.6 %shard_map.86 = (bf16[256,4096]{1,0:T(8,128)(2,1)}, f32[24,2048]{1,0:T(8,128)}, f32[24,2048]{1,0:T(8,128)}) custom-call(bf16[256,4096]{1,0:T(8,128)(2,1)} %copy-done, f32[24,2048]{1,0:T(8,128)} %copy-done.1, f32[24,2048]{1,0:T(8,128)} %copy-done.2), custom_call_target="tpu_custom_call" | custom-call | tf_op jit(solution)/shard_map/pallas_call | solution.py:438
Async XLA Ops:
  63.7 1.3 copy-start
  65.0 0.7 copy-start.1
  65.7 0.7 copy-start.2

commit v7 on v6

--- a/solution.py
+++ b/solution.py
@@ -168,7 +168,7 @@
 
         loop(cap, point)
 
-    def backward(h, between=None):
+    def backward(h):
         at = pl.ds(h * half, half)
 
         def make(s):
@@ -183,9 +183,6 @@
             dpre[s, at, :] = (scan[table[END_COL, s]] * gate[s, at, :]).astype(BF)
 
         loop(cap, point)
-        if between is not None:
-            between()
-
         def make_term(s):
             return dot(dpre[s, at, :], win[s], 1, 1)
 
@@ -334,19 +331,16 @@
     y_out(0)
     pass_on(1, 1)
     settle(1, 1)
-    for n in range(n_c):
-        wgrad(1, n)
-
-    def between():
-        for n in range(n_c):
-            z_out(1, n)
-            wgrad(0, n)
-
-    backward(1, between)
+    backward(1)
     exchange(1).start()
-    z_out(0, 0)
+    wgrad(1, 0)
     y_out(1)
     for n in range(1, n_c):
+        wgrad(1, n)
+    for n in range(n_c):
+        z_out(1, n)
+        wgrad(0, n)
+    for n in range(n_c):
         z_out(0, n)
     y_in(0)
     for n in range(n_c):
@@ -441,6 +435,7 @@
         in_specs=[any_space] * 3,
         out_specs=(any_space,) * 3,
         scratch_shapes=[dma((6,))],
+        compiler_params=pltpu.CompilerParams(vmem_limit_bytes=4 * 1024 * 1024),
     )(*results)
 
 

time: 143 us -> 62.8 us (0.44)
  Pallas kernels: 140 us -> 62 us
  local copies, waits for them, and re-layouts: 2.67 us -> 0 us
    pallas_call x1, Pallas kernels: 76.6 us -> 1.49 us  [local(): pl.pallas_call(hand_over, out_shape=tuple((jax.ShapeDtypeStruct(v.shape,...]
    unnamed x6 -> x0, local copies, waits for them, and re-layouts: 2.67 us -> none
    pallas_call x1, Pallas kernels: 63 us -> 60.5 us  [local(): pl.pallas_call(functools.partial(kernel, n_dp, n_t, chunk), out_shape=sha...]
where the time goes in v7:
time: 62.8 us; the launch traced here: 62.6 us
  Pallas kernels  62 us (99%)
  between operations  0.64 us (1%)
    pallas_call x1, Pallas kernels, local(): pl.pallas_call(functools.partial(kernel, n_dp, n_t, chunk), out_shape=sha...  60.5 us
    pallas_call x1, Pallas kernels, local(): pl.pallas_call(hand_over, out_shape=tuple((jax.ShapeDtypeStruct(v.shape,...  1.49 us

profile of v7, /device:TPU:0, one launch (start us, length us, event | category | flops | bytes accessed | tf_op | source)
XLA Modules:
  0.0 62.6 jit_solution(9332404131692478789)
XLA Ops:
  0.6 60.5 %shard_map.85 = (bf16[256,4096]{1,0:T(8,128)(2,1)S(1)}, f32[24,2048]{1,0:T(8,128)S(1)}, f32[24,2048]{1,0:T(8,128)S(1)}) custom-call(s32[1,24]{1,0:T(1,128)} %rows.1, s32[1,24]{1,0:T(1,128)} %cols.1, bf16[256,1024]{1,0:T(8,128)(2,1)} %tok_hbm.1, bf16[256,1024]{1,0:T(8,128)(2,1)} %grad_hbm.1, bf16[24,128,128]{2,1,0:T(8,128)(2,1)} %win_hbm.1, ...), custom_call_target="tpu_custom_call" | custom-call | flops 1006632960 | bytes 8388608 | tf_op jit(solution)/shard_map/pallas_call | solution.py:417
  61.1 1.5 %shard_map.86 = (bf16[256,4096]{1,0:T(8,128)(2,1)}, f32[24,2048]{1,0:T(8,128)}, f32[24,2048]{1,0:T(8,128)}) custom-call(bf16[256,4096]{1,0:T(8,128)(2,1)S(1)} %get-tuple-element.6.dx, f32[24,2048]{1,0:T(8,128)S(1)} %get-tuple-element.7.gin, f32[24,2048]{1,0:T(8,128)S(1)} %get-tuple-element.8.gout), custom_call_target="tpu_custom_call" | custom-call | tf_op jit(solution)/shard_map/pallas_call | solution.py:432

commit v8 on v6

--- a/solution.py
+++ b/solution.py
@@ -10,7 +10,7 @@
 MESH = pl.DeviceIdType.MESH
 BF, F32, I32 = jnp.bfloat16, jnp.float32, jnp.int32
 CLIP = 4.0
-UNROLL = 4
+UNROLL, AHEAD = 8, 4
 PREV_COL, END_COL, ROW, LIVE, PREV_ROW, LAST = range(6)
 
 
@@ -30,9 +30,11 @@
 def loop_pairs(count, make, use):
     def outer(g, carry):
         at = [g * UNROLL + u for u in range(UNROLL)]
-        made = [make(i) for i in at]
-        for i, value in zip(at, made):
-            use(i, value)
+        made = [make(i) for i in at[:AHEAD]]
+        for n, i in enumerate(at):
+            use(i, made[n])
+            if n + AHEAD < UNROLL:
+                made.append(make(at[n + AHEAD]))
         return carry
 
     lax.fori_loop(0, count // UNROLL, outer, 0)
@@ -336,19 +338,18 @@
     settle(1, 1)
     for n in range(n_c):
         wgrad(1, n)
-
-    def between():
-        for n in range(n_c):
-            z_out(1, n)
-            wgrad(0, n)
-
-    backward(1, between)
+    backward(1, lambda: z_out(1, 0))
     exchange(1).start()
+    for n in range(n_c):
+        wgrad(0, n)
+        if n == 0:
+            y_out(1)
+        if n + 1 < n_c:
+            z_out(1, n + 1)
     z_out(0, 0)
-    y_out(1)
+    y_in(0)
     for n in range(1, n_c):
         z_out(0, n)
-    y_in(0)
     for n in range(n_c):
         z_in(1, n)
     y_in(1)
@@ -441,6 +442,7 @@
         in_specs=[any_space] * 3,
         out_specs=(any_space,) * 3,
         scratch_shapes=[dma((6,))],
+        compiler_params=pltpu.CompilerParams(vmem_limit_bytes=4 * 1024 * 1024),
     )(*results)
 
 

time: 143 us -> 59.6 us (0.42)
  Pallas kernels: 140 us -> 58.8 us
  local copies, waits for them, and re-layouts: 2.67 us -> 0 us
    pallas_call x1, Pallas kernels: 76.6 us -> 1.49 us  [local(): pl.pallas_call(hand_over, out_shape=tuple((jax.ShapeDtypeStruct(v.shape,...]
    pallas_call x1, Pallas kernels: 63 us -> 57.3 us  [local(): pl.pallas_call(functools.partial(kernel, n_dp, n_t, chunk), out_shape=sha...]
    unnamed x6 -> x0, local copies, waits for them, and re-layouts: 2.67 us -> none
where the time goes in v8:
time: 59.6 us; the launch traced here: 59.4 us
  Pallas kernels  58.8 us (99%)
  between operations  0.64 us (1%)
    pallas_call x1, Pallas kernels, local(): pl.pallas_call(functools.partial(kernel, n_dp, n_t, chunk), out_shape=sha...  57.3 us
    pallas_call x1, Pallas kernels, local(): pl.pallas_call(hand_over, out_shape=tuple((jax.ShapeDtypeStruct(v.shape,...  1.49 us

profile of v8, /device:TPU:0, one launch (start us, length us, event | category | flops | bytes accessed | tf_op | source)
XLA Modules:
  0.0 59.4 jit_solution(3151612933616788404)
XLA Ops:
  0.6 57.3 %shard_map.85 = (bf16[256,4096]{1,0:T(8,128)(2,1)S(1)}, f32[24,2048]{1,0:T(8,128)S(1)}, f32[24,2048]{1,0:T(8,128)S(1)}) custom-call(s32[1,24]{1,0:T(1,128)} %rows.1, s32[1,24]{1,0:T(1,128)} %cols.1, bf16[256,1024]{1,0:T(8,128)(2,1)} %tok_hbm.1, bf16[256,1024]{1,0:T(8,128)(2,1)} %grad_hbm.1, bf16[24,128,128]{2,1,0:T(8,128)(2,1)} %win_hbm.1, ...), custom_call_target="tpu_custom_call" | custom-call | flops 1006632960 | bytes 8388608 | tf_op jit(solution)/shard_map/pallas_call | solution.py:424
  57.9 1.5 %shard_map.86 = (bf16[256,4096]{1,0:T(8,128)(2,1)}, f32[24,2048]{1,0:T(8,128)}, f32[24,2048]{1,0:T(8,128)}) custom-call(bf16[256,4096]{1,0:T(8,128)(2,1)S(1)} %get-tuple-element.6.dx, f32[24,2048]{1,0:T(8,128)S(1)} %get-tuple-element.7.gin, f32[24,2048]{1,0:T(8,128)S(1)} %get-tuple-element.8.gout), custom_call_target="tpu_custom_call" | custom-call | tf_op jit(solution)/shard_map/pallas_call | solution.py:439
